TPU v7x, 32 devices: a whole 2x2x4 slice. The times are simulated.
32 devices in a mesh: gx: 4 (over x, core), gy: 8 (over z, y).
Axes of the slice: x: 2, y: 2, z: 4, core: 2. Of those that a mesh axis runs over, the one named last changes fastest.
Arguments:
- cell_power: float32 [6144, 2048], P(('gx', 'gy')), may hold values from 0.5 to 20
- cell_bin: int32 [6144, 2048], P(('gx', 'gy')), may hold values from 0 to 2047
- block_owner: int32 [6144, 1], P(('gx', 'gy')), may hold values from 0 to 31; in each aligned block of 192 rows (0 to 191, 192 to 383, ...) at most 9 rows name the same one
- block_tile: int32 [6144], P(('gx', 'gy')), may hold values from 0 to 7
- temp_prev: float32 [8, 512, 1024], P(None, 'gx', 'gy'), may hold values from -6 to 6
- cond_x: float32 [8, 512, 1024], P(None, 'gx', 'gy'), may hold values from 0.5 to 4
- cond_y: float32 [8, 512, 1024], P(None, 'gx', 'gy'), may hold values from 0.5 to 4
- cond_z: float32 [8, 512, 1024], P(None, 'gx', 'gy'), may hold values from 1 to 8
- weight: float32 [8, 512, 1024], P(None, 'gx', 'gy'), may hold values from 0.2 to 2
Outputs:
- temperature: float32 [8, 512, 1024], P(None, 'gx', 'gy')
- cell_grad: float32 [2, 6144, 2048], P(None, ('gx', 'gy'))
Inputs may be any that keep to these rules, and one draw needn't show every extreme that they name: `block_owner`: among the blocks of one device, at most 9 name the same owner, a bound that some of them reach. `cell_bin`: A bin is the row within the tile times 128 plus the column.
All inputs are finite; a program needn't handle non-finite values.
Results may differ from a plain program's by a relative error of at most 0.00012.
Values sent between devices are 32-bit elements; how exact they have to be, the bound alone decides.
A program may use at most 128 MiB of HBM per device.

v0:
```python
import jax
import jax.numpy as jnp
from jax import lax
from jax.sharding import PartitionSpec as P

TROWS = 16


def shifted(block, axis, distance):
    devices = range(lax.axis_size(axis))
    route = [(i - distance, i) for i in devices if i - distance in devices]
    return lax.ppermute(block, axis, route)


def with_halo(array, sides, width):
    for axis, dim in sides:
        peers, length = (lax.axis_size(axis), array.shape[dim])
        up = [(i, (i + 1) % peers) for i in range(peers - 1)]
        down = [(j, i) for i, j in up]
        last = lax.slice_in_dim(array, length - width, length, axis=dim)
        initial = lax.slice_in_dim(array, 0, width, axis=dim)
        before = lax.ppermute(last, axis, up)
        after = lax.ppermute(initial, axis, down)
        array = jnp.concatenate([before, array, after], axis=dim)
    return array


def neighbours(faces, padded):
    east, west, north, south, upward, downward = faces
    centre = padded[:, 1:-1, 1:-1]
    above = jnp.concatenate([centre[1:], jnp.zeros_like(centre[:1])], axis=0)
    below = jnp.concatenate([jnp.zeros_like(centre[:1]), centre[:-1]], axis=0)
    return (
        east * padded[:, 2:, 1:-1]
        + west * padded[:, :-2, 1:-1]
        + north * padded[:, 1:-1, 2:]
        + south * padded[:, 1:-1, :-2]
        + upward * above
        + downward * below
    )


def on_device(
    cell_power, cell_bin, block_owner, block_tile, temp_prev, cond_x, cond_y, cond_z, weight
):
    block_count, block_cells = cell_power.shape
    layers, dev_rows, dev_cols = temp_prev.shape
    tile_count = dev_rows // TROWS
    tile_bins = TROWS * dev_cols
    devices = lax.axis_size(("gx", "gy"))
    size_gx = lax.axis_size("gx")
    size_gy = lax.axis_size("gy")
    capacity = max(2, 3 * block_count // (2 * devices))
    slot_count = devices * capacity
    highest = lax.Precision.HIGHEST
    bin_rows = cell_bin // dev_cols
    bin_cols = cell_bin % dev_cols
    row_iota = jnp.arange(TROWS, dtype=jnp.int32)
    col_iota = jnp.arange(dev_cols, dtype=jnp.int32)
    groups = block_count // 8

    def bin_group(operands):
        powers, rows_in, cols_in = operands
        row_hot = (rows_in[:, None, :] == row_iota[None, :, None]).astype(jnp.float32) * powers[
            :, None, :
        ]
        col_hot = (cols_in[:, None, :] == col_iota[None, :, None]).astype(jnp.float32)
        return jnp.einsum("kxc,kyc->kxy", row_hot, col_hot, precision=highest)

    tile_maps = lax.map(
        bin_group,
        (
            cell_power.reshape(groups, 8, block_cells),
            bin_rows.reshape(groups, 8, block_cells),
            bin_cols.reshape(groups, 8, block_cells),
        ),
    )
    tile_maps = tile_maps.reshape(block_count, tile_bins)
    owner = block_owner[:, 0]
    owner_hot = (owner[:, None] == jnp.arange(devices, dtype=jnp.int32)[None, :]).astype(jnp.int32)
    earlier = jnp.cumsum(owner_hot, axis=0) - owner_hot
    rank = jnp.sum(earlier * owner_hot, axis=1)
    slot = owner * capacity + rank
    send_maps = jnp.zeros((slot_count, tile_bins), jnp.float32).at[slot].set(tile_maps)
    send_tiles = (
        jnp.full((slot_count,), -1.0, jnp.float32).at[slot].set(block_tile.astype(jnp.float32))
    )
    got_maps, got_tiles = (
        lax.all_to_all(
            send_maps.reshape(devices, capacity, tile_bins),
            ("gx", "gy"),
            split_axis=0,
            concat_axis=0,
            tiled=True,
        ),
        lax.all_to_all(
            send_tiles.reshape(devices, capacity),
            ("gx", "gy"),
            split_axis=0,
            concat_axis=0,
            tiled=True,
        ),
    )
    got_maps = got_maps.reshape(slot_count, tile_bins)
    got_tiles = got_tiles.reshape(slot_count)
    picker = (got_tiles[None, :] == jnp.arange(tile_count, dtype=jnp.float32)[:, None]).astype(
        jnp.float32
    )
    power_tiles = jnp.dot(picker, got_maps, precision=highest)
    source_map = power_tiles.reshape(1, dev_rows, dev_cols)
    margin = 1
    west_rim = shifted(cond_x[:, -1:, :], "gx", 1)
    south_rim = shifted(cond_y[:, :, -1:], "gy", 1)
    west = jnp.concatenate([west_rim, cond_x[:, :-1, :]], axis=1)
    south = jnp.concatenate([south_rim, cond_y[:, :, :-1]], axis=2)
    downward = jnp.concatenate([jnp.zeros_like(cond_z[:1]), cond_z[:-1]], axis=0)
    faces = (cond_x, west, cond_y, south, cond_z, downward)
    inner = margin - 1
    global_rows = (
        lax.axis_index("gx") * dev_rows - inner + jnp.arange(dev_rows + 2 * inner, dtype=jnp.int32)
    )
    global_cols = (
        lax.axis_index("gy") * dev_cols - inner + jnp.arange(dev_cols + 2 * inner, dtype=jnp.int32)
    )
    inside = ((global_rows >= 0) & (global_rows < dev_rows * size_gx))[:, None] & (
        (global_cols >= 0) & (global_cols < dev_cols * size_gy)
    )[None, :]
    raw_diag = faces[0] + faces[1] + faces[2] + faces[3] + faces[4] + faces[5]
    diag = jnp.where(inside[None], raw_diag, 1.0)
    sweep = temp_prev
    for turn in range(3):
        padded = with_halo(sweep, (("gx", 1), ("gy", 2)), 1)
        summed = neighbours(faces, padded)
        summed = summed.at[0].add(source_map[0])
        sweep = summed / diag
    adjoint = weight * sweep / diag
    rims_total = None
    for turn in range(3):
        adjoint_padded = with_halo(adjoint, (("gx", 1), ("gy", 2)), 1)
        rims_total = adjoint_padded if rims_total is None else rims_total + adjoint_padded
        if turn < 2:
            adjoint = neighbours(faces, adjoint_padded) / diag
    surface = rims_total[0]
    slope_x = 0.5 * (surface[2:, 1:-1] - surface[:-2, 1:-1])
    slope_y = 0.5 * (surface[1:-1, 2:] - surface[1:-1, :-2])
    payload = jnp.stack(
        [slope_x.reshape(tile_count, tile_bins), slope_y.reshape(tile_count, tile_bins)], axis=1
    )
    payload = payload.reshape(tile_count, 2 * tile_bins)
    width = payload.shape[1]
    back_slots = jnp.dot(picker.T, payload, precision=highest)
    returned = lax.all_to_all(
        back_slots.reshape(devices, capacity, width),
        ("gx", "gy"),
        split_axis=0,
        concat_axis=0,
        tiled=True,
    )
    returned = returned.reshape(slot_count, width)
    picked_slots = returned[slot]
    block_slopes = picked_slots.reshape(block_count, 2, TROWS, dev_cols)

    def cell_group(operands):
        slopes, powers, rows_in, cols_in = operands
        col_hot = (cols_in[:, None, :] == col_iota[None, :, None]).astype(jnp.float32)
        row_hot = (rows_in[:, None, :] == row_iota[None, :, None]).astype(jnp.float32)
        spread = jnp.einsum("kaxy,kyc->kaxc", slopes, col_hot, precision=highest)
        picked = jnp.sum(spread * row_hot[:, None], axis=2)
        return picked * powers[:, None, :]

    grads = lax.map(
        cell_group,
        (
            block_slopes.reshape(groups, 8, 2, TROWS, dev_cols),
            cell_power.reshape(groups, 8, block_cells),
            bin_rows.reshape(groups, 8, block_cells),
            bin_cols.reshape(groups, 8, block_cells),
        ),
    )
    grads = grads.reshape(block_count, 2, block_cells)
    return (sweep, jnp.transpose(grads, (1, 0, 2)))


def solution(mesh):
    return jax.shard_map(
        on_device,
        mesh=mesh,
        in_specs=(
            P(("gx", "gy"), None),
            P(("gx", "gy"), None),
            P(("gx", "gy"), None),
            P(("gx", "gy")),
            P(None, "gx", "gy"),
            P(None, "gx", "gy"),
            P(None, "gx", "gy"),
            P(None, "gx", "gy"),
            P(None, "gx", "gy"),
        ),
        out_specs=(P(None, "gx", "gy"), P(None, ("gx", "gy"), None)),
        check_vma=False,
    )
```

profile of v0, /device:TPU:0, one launch (start us, length us, event | category | flops | bytes accessed | tf_op | source)
XLA Modules:
  0.0 746.9 jit_solution(3343747404256114060)
XLA Ops:
  6.2 7.3 all-to-all-start
  16.3 131.9 %while.25 = (s32[]{:T(128)}, f32[24,8,16,128]{3,2,1,0:T(8,128)}, s32[24,8,2048]{2,1,0:T(8,128)S(1)}, f32[24,8,2048]{2,1,0:T(8,128)}, s32[24,8,2048]{2,1,0:T(8,128)S(1)}, /*index=5*/s32[]{:T(128)}) while((s32[]{:T(128)}, f32[24,8,16,128]{3,2,1,0:T(8,128)}, s32[24,8,2048]{2,1,0:T(8,128)S(1)}, f32[24,8,2048]{2,1,0:T(8,128)}, ...), condition=%wide.region_5.6_spmd.clone, body=%wide.region_4.5_spmd.clone.sunk | while | flops 405274624 | bytes 655949 | solution.py:70
  17.2 4.6 fusion.117
  22.7 4.6 fusion.117
  28.1 4.6 fusion.117
  33.6 4.6 fusion.117
  39.1 4.6 fusion.117
  44.6 4.6 fusion.117
  50.1 4.6 fusion.117
  55.6 4.6 fusion.117
  61.1 4.6 fusion.117
  66.6 4.6 fusion.117
  72.1 4.6 fusion.117
  77.6 4.6 fusion.117
  83.1 4.6 fusion.117
  88.6 4.6 fusion.117
  94.1 4.6 fusion.117
  99.6 4.6 fusion.117
  105.1 4.6 fusion.117
  110.6 4.6 fusion.117
  116.1 4.6 fusion.117
  121.5 4.6 fusion.117
  127.0 4.6 fusion.117
  132.5 4.6 fusion.117
  138.0 4.6 fusion.117
  143.5 4.6 fusion.117
  156.2 6.0 all-to-all-start.1
  180.9 4.7 collective-permute-start.5
  192.4 65.7 %all-to-all-done.1 = f32[32,9,2048]{2,1,0:T(8,128)} async-done(((f32[32,9,2048]{2,1,0:T(8,128)}), f32[32,9,2048]{2,1,0:T(8,128)}, u32[]{:S(2)}, u32[]{:S(2)}) %all-to-all-start.1) | async-done | bytes 2359328 | tf_op jit(solution)/shard_map/all_to_all | solution.py:89
  274.3 4.5 collective-permute-start.9
  287.0 7.9 %collective-permute-start.11 = (f32[8,1,128]{1,0,2:T(8,128)}, f32[8,1,128]{1,0,2:T(8,128)}, u32[]{:S(2)}, u32[]{:S(2)}) collective-permute-start(f32[8,1,128]{1,0,2:T(8,128)} %get-tuple-element.233), channel_id=1, source_target_pairs={{0,8},{8,16},{16,24},{1,9},{9,17},{17,25},{2,10},{10,18},{18,26},{... | collective-permute-start | bytes 12296 | tf_op jit(solution)/shard_map/ppermute | solution.py:22
  299.0 4.5 collective-permute-start.13
  313.5 8.6 %collective-permute-start.14 = (f32[8,1,128]{1,0,2:T(8,128)S(1)}, f32[8,1,128]{1,0,2:T(8,128)S(1)}, u32[]{:S(2)}, u32[]{:S(2)}) collective-permute-start(f32[8,1,128]{1,0,2:T(8,128)S(1)} %get-tuple-element.229), channel_id=1, source_target_pairs={{0,8},{8,16},{16,24},{1,9},{9,17},{17,25},{2,10},{10,18},{18,26},{... | collective-permute-start | bytes 12296 | tf_op jit(solution)/shard_map/ppermute | solution.py:22
  323.6 5.3 collective-permute-done.15
  328.9 4.8 collective-permute-start.16
  335.1 5.3 collective-permute-done.17
  341.5 8.0 %collective-permute-start.18 = (f32[8,1,128]{1,0,2:T(8,128)S(1)}, f32[8,1,128]{1,0,2:T(8,128)S(1)}, u32[]{:S(2)}, u32[]{:S(2)}) collective-permute-start(f32[8,1,128]{1,0,2:T(8,128)S(1)} %get-tuple-element.225), channel_id=1, source_target_pairs={{0,8},{8,16},{16,24},{1,9},{9,17},{17,25},{2,10},{10,18},{18,26},{... | collective-permute-start | bytes 12296 | tf_op jit(solution)/shard_map/ppermute | solution.py:22
  353.9 4.8 collective-permute-start.20
  360.1 4.2 collective-permute-done.21
  365.3 7.8 %collective-permute-start.22 = (f32[8,1,128]{1,0,2:T(8,128)S(1)}, f32[8,1,128]{1,0,2:T(8,128)S(1)}, u32[]{:S(2)}, u32[]{:S(2)}) collective-permute-start(f32[8,1,128]{1,0,2:T(8,128)S(1)} %get-tuple-element.221), channel_id=1, source_target_pairs={{0,8},{8,16},{16,24},{1,9},{9,17},{17,25},{2,10},{10,18},{18,26},{... | collective-permute-start | bytes 12296 | tf_op jit(solution)/shard_map/ppermute | solution.py:22
  377.8 4.1 collective-permute-start.24
  383.5 3.9 collective-permute-done.25
  392.7 6.3 copy.101
  399.0 12.0 %all-to-all-start.2 = ((f32[32,9,4096]{2,1,0:T(8,128)}), f32[32,9,4096]{2,1,0:T(8,128)}, u32[]{:S(2)}, u32[]{:S(2)}) async-start(f32[32,9,4096]{2,1,0:T(8,128)} %copy.101), calls=%async_computation.2 | async-start | bytes 16777216 | tf_op jit(solution)/shard_map/all_to_all | solution.py:152
  412.1 188.2 %all-to-all-done.2 = f32[32,9,4096]{2,1,0:T(8,128)} async-done(((f32[32,9,4096]{2,1,0:T(8,128)}), f32[32,9,4096]{2,1,0:T(8,128)}, u32[]{:S(2)}, u32[]{:S(2)}) %all-to-all-start.2) | async-done | bytes 4718624 | tf_op jit(solution)/shard_map/all_to_all | solution.py:152
  600.3 6.1 reshape.228
  606.4 5.4 gather_fusion
  611.8 135.0 %while.26 = (s32[]{:T(128)}, f32[24,8,2,2048]{3,1,0,2:T(8,128)}, f32[24,8,2,16,128]{4,1,3,2,0:T(8,128)S(1)}, s32[24,8,2048]{2,1,0:T(8,128)}, s32[24,8,2048]{2,1,0:T(8,128)}, /*index=5*/f32[24,8,2048]{2,1,0:T(8,128)}, s32[]{:T(128)}) while((s32[]{:T(128)}, f32[24,8,2,2048]{3,1,0,2:T(8,128)}, f32[24,8,2,16,128]{4,1,3,2,0:T(8,128)S(1)}, ...), condition=%wide.region_9.10_spmd.clone, body=%wide.region_7.9_spmd.clone.sunk | while | flops 808976384 | bytes 3736153 | solution.py:171
  (383 shorter events, 258.0 us)
Async XLA Ops:
  6.2 150.0 %all-to-all-start = ((f32[32,1,9]{2,1,0:T(1,128)}), f32[32,1,9]{2,1,0:T(1,128)S(1)}, u32[]{:S(2)}, u32[]{:S(2)}) async-start(f32[32,1,9]{2,1,0:T(1,128)} %bitcast.4), calls=%async_computation | async-start | bytes 32768 | tf_op jit(solution)/shard_map/all_to_all | solution.py:96
  156.2 6.0 copy-start.23
  156.2 9.8 %copy-start.21 = (f32[8,128,128]{2,1,0:T(8,128)S(1)}, f32[8,128,128]{2,1,0:T(8,128)}, u32[]{:S(2)}) copy-start(f32[8,128,128]{2,1,0:T(8,128)} %param.23) | copy-start | bytes 1572868
  156.2 101.9 %all-to-all-start.1 = ((f32[32,9,2048]{2,1,0:T(8,128)}), f32[32,9,2048]{2,1,0:T(8,128)}, u32[]{:S(2)}, u32[]{:S(2)}) async-start(f32[32,9,2048]{2,1,0:T(8,128)} %reshape.224), calls=%async_computation.1 | async-start | bytes 8388608 | tf_op jit(solution)/shard_map/all_to_all | solution.py:89
  162.4 26.1 %collective-permute-start.4 = (f32[8,128,1]{1,0,2:T(8,128)S(1)}, f32[8,128,1]{1,0,2:T(8,128)S(1)}, u32[]{:S(2)}, u32[]{:S(2)}) collective-permute-start(f32[8,128,1]{1,0,2:T(8,128)S(1)} %slice.360), channel_id=1, source_target_pairs={{0,1},{1,2},{2,3},{3,4},{4,5},{5,6},{6,7},{8,9},{9,10},{10,11},{11... | collective-permute-start | bytes 12296 | tf_op jit(solution)/shard_map/ppermute | solution.py:12
  167.1 12.3 %collective-permute-start = (f32[8,1,128]{1,0,2:T(8,128)}, f32[8,1,128]{1,0,2:T(8,128)S(1)}, u32[]{:S(2)}, u32[]{:S(2)}) collective-permute-start(f32[8,1,128]{1,0,2:T(8,128)} %copy.61), channel_id=1, source_target_pairs={{8,0},{16,8},{24,16},{9,1},{17,9},{25,17},{10,2},{18,10},{26,18},{... | collective-permute-start | bytes 12296 | tf_op jit(solution)/shard_map/ppermute | solution.py:23
  169.4 10.0 %collective-permute-start.2 = (f32[8,1,128]{1,0,2:T(8,128)}, f32[8,1,128]{1,0,2:T(8,128)S(1)}, u32[]{:S(2)}, u32[]{:S(2)}) collective-permute-start(f32[8,1,128]{1,0,2:T(8,128)} %copy.66), channel_id=1, source_target_pairs={{0,8},{8,16},{16,24},{1,9},{9,17},{17,25},{2,10},{10,18},{18,26},{... | collective-permute-start | bytes 12296 | tf_op jit(solution)/shard_map/ppermute | solution.py:22
  174.3 14.3 %collective-permute-start.1 = (f32[8,1,128]{1,0,2:T(8,128)}, f32[8,1,128]{1,0,2:T(8,128)}, u32[]{:S(2)}, u32[]{:S(2)}) collective-permute-start(f32[8,1,128]{1,0,2:T(8,128)} %copy.64), channel_id=1, source_target_pairs={{0,8},{8,16},{16,24},{1,9},{9,17},{17,25},{2,10},{10,18},{18,26},{... | collective-permute-start | bytes 12296 | tf_op jit(solution)/shard_map/ppermute | solution.py:12
  179.3 6.4 copy-start.22
  179.4 6.3 copy-start.16
  179.4 6.3 copy-start.17
  179.5 9.1 %collective-permute-start.3 = (f32[8,130,1]{1,0,2:T(8,128)S(1)}, f32[8,130,1]{1,0,2:T(8,128)S(1)}, u32[]{:S(2)}, u32[]{:S(2)}) collective-permute-start(f32[8,130,1]{1,0,2:T(8,128)S(1)} %get-tuple-element.219), channel_id=1, source_target_pairs={{1,0},{2,1},{3,2},{4,3},{5,4},{6,5},{7,6},{9,8},{10,9},{11,10},{12... | collective-permute-start | bytes 12488 | tf_op jit(solution)/shard_map/ppermute | solution.py:23
  180.9 7.7 %collective-permute-start.5 = (f32[8,130,1]{1,0,2:T(8,128)S(1)}, f32[8,130,1]{1,0,2:T(8,128)S(1)}, u32[]{:S(2)}, u32[]{:S(2)}) collective-permute-start(f32[8,130,1]{1,0,2:T(8,128)S(1)} %get-tuple-element.220), channel_id=1, source_target_pairs={{0,1},{1,2},{2,3},{3,4},{4,5},{5,6},{6,7},{8,9},{9,10},{10,11},{11... | collective-permute-start | bytes 12488 | tf_op jit(solution)/shard_map/ppermute | solution.py:22
  192.4 112.5 %copy-start = (f32[8,128,128]{1,0,2:T(8,128)}, f32[8,128,128]{1,0,2:T(8,128)S(1)}, u32[]{:S(2)}) copy-start(f32[8,128,128]{1,0,2:T(8,128)S(1)} %get-tuple-element.202) | copy-start | bytes 1572868
  267.0 4.4 collective-permute-start.6
  268.3 4.6 collective-permute-start.7
  273.0 5.9 collective-permute-start.8
  274.3 5.9 collective-permute-start.9
  285.7 11.3 %collective-permute-start.10 = (f32[8,1,128]{1,0,2:T(8,128)}, f32[8,1,128]{1,0,2:T(8,128)}, u32[]{:S(2)}, u32[]{:S(2)}) collective-permute-start(f32[8,1,128]{1,0,2:T(8,128)} %get-tuple-element.234), channel_id=1, source_target_pairs={{8,0},{16,8},{24,16},{9,1},{17,9},{25,17},{10,2},{18,10},{26,18},{... | collective-permute-start | bytes 12296 | tf_op jit(solution)/shard_map/ppermute | solution.py:23
  287.0 10.0 %collective-permute-start.11 = (f32[8,1,128]{1,0,2:T(8,128)}, f32[8,1,128]{1,0,2:T(8,128)}, u32[]{:S(2)}, u32[]{:S(2)}) collective-permute-start(f32[8,1,128]{1,0,2:T(8,128)} %get-tuple-element.233), channel_id=1, source_target_pairs={{0,8},{8,16},{16,24},{1,9},{9,17},{17,25},{2,10},{10,18},{18,26},{... | collective-permute-start | bytes 12296 | tf_op jit(solution)/shard_map/ppermute | solution.py:22
  297.7 5.9 collective-permute-start.12
  299.0 5.9 collective-permute-start.13
  313.5 10.1 %collective-permute-start.14 = (f32[8,1,128]{1,0,2:T(8,128)S(1)}, f32[8,1,128]{1,0,2:T(8,128)S(1)}, u32[]{:S(2)}, u32[]{:S(2)}) collective-permute-start(f32[8,1,128]{1,0,2:T(8,128)S(1)} %get-tuple-element.229), channel_id=1, source_target_pairs={{0,8},{8,16},{16,24},{1,9},{9,17},{17,25},{2,10},{10,18},{18,26},{... | collective-permute-start | bytes 12296 | tf_op jit(solution)/shard_map/ppermute | solution.py:22
  322.1 18.4 %copy-start.1 = (f32[8,128,128]{1,0,2:T(8,128)S(1)}, f32[8,128,128]{1,0,2:T(8,128)}, u32[]{:S(2)}) copy-start(f32[8,128,128]{1,0,2:T(8,128)} %copy-done) | copy-start | bytes 1572868
  322.1 18.4 %copy-start.3 = (f32[8,128,128]{1,0,2:T(8,128)S(1)}, f32[8,128,128]{1,0,2:T(8,128)}, u32[]{:S(2)}) copy-start(f32[8,128,128]{1,0,2:T(8,128)} %get-tuple-element.200) | copy-start | bytes 1572868
  322.1 6.7 collective-permute-start.15
  323.6 16.9 %copy-start.4 = (f32[8,1,128]{1,0,2:T(8,128)}, f32[8,1,128]{1,0,2:T(8,128)S(1)}, u32[]{:S(2)}) copy-start(f32[8,1,128]{1,0,2:T(8,128)S(1)} %collective-permute-done.14) | copy-start | bytes 12292
  328.8 11.6 %copy-start.6 = (f32[8,1,128]{1,0,2:T(8,128)}, f32[8,1,128]{1,0,2:T(8,128)S(1)}, u32[]{:S(2)}) copy-start(f32[8,1,128]{1,0,2:T(8,128)S(1)} %collective-permute-done.15) | copy-start | bytes 12292
  328.9 6.2 collective-permute-start.16
  333.7 6.7 collective-permute-start.17
  341.5 9.5 %collective-permute-start.18 = (f32[8,1,128]{1,0,2:T(8,128)S(1)}, f32[8,1,128]{1,0,2:T(8,128)S(1)}, u32[]{:S(2)}, u32[]{:S(2)}) collective-permute-start(f32[8,1,128]{1,0,2:T(8,128)S(1)} %get-tuple-element.225), channel_id=1, source_target_pairs={{0,8},{8,16},{16,24},{1,9},{9,17},{17,25},{2,10},{10,18},{18,26},{... | collective-permute-start | bytes 12296 | tf_op jit(solution)/shard_map/ppermute | solution.py:22
  349.5 4.3 collective-permute-start.19
  351.0 13.2 %copy-start.8 = (f32[8,1,128]{1,0,2:T(8,128)}, f32[8,1,128]{1,0,2:T(8,128)S(1)}, u32[]{:S(2)}) copy-start(f32[8,1,128]{1,0,2:T(8,128)S(1)} %collective-permute-done.18) | copy-start | bytes 12292
  353.8 10.4 %copy-start.10 = (f32[8,1,128]{1,0,2:T(8,128)}, f32[8,1,128]{1,0,2:T(8,128)S(1)}, u32[]{:S(2)}) copy-start(f32[8,1,128]{1,0,2:T(8,128)S(1)} %collective-permute-done.19) | copy-start | bytes 12292
  353.9 6.2 collective-permute-start.20
  358.7 5.5 collective-permute-start.21
  365.1 12.7 %copy-start.2 = (f32[8,128,128]{1,0,2:T(8,128)}, f32[8,128,128]{1,0,2:T(8,128)S(1)}, u32[]{:S(2)}) copy-start(f32[8,128,128]{1,0,2:T(8,128)S(1)} %fusion.40) | copy-start | bytes 1572868
  365.1 22.3 %copy-start.5 = (f32[8,1,128]{1,0,2:T(8,128)S(1)}, f32[8,1,128]{1,0,2:T(8,128)}, u32[]{:S(2)}) copy-start(f32[8,1,128]{1,0,2:T(8,128)} %copy-done.4) | copy-start | bytes 12292
  365.1 22.3 %copy-start.7 = (f32[8,1,128]{1,0,2:T(8,128)S(1)}, f32[8,1,128]{1,0,2:T(8,128)}, u32[]{:S(2)}) copy-start(f32[8,1,128]{1,0,2:T(8,128)} %copy-done.6) | copy-start | bytes 12292
  365.1 22.3 %copy-start.9 = (f32[8,1,128]{1,0,2:T(8,128)S(1)}, f32[8,1,128]{1,0,2:T(8,128)}, u32[]{:S(2)}) copy-start(f32[8,1,128]{1,0,2:T(8,128)} %copy-done.8) | copy-start | bytes 12292
  365.3 9.3 %collective-permute-start.22 = (f32[8,1,128]{1,0,2:T(8,128)S(1)}, f32[8,1,128]{1,0,2:T(8,128)S(1)}, u32[]{:S(2)}, u32[]{:S(2)}) collective-permute-start(f32[8,1,128]{1,0,2:T(8,128)S(1)} %get-tuple-element.221), channel_id=1, source_target_pairs={{0,8},{8,16},{16,24},{1,9},{9,17},{17,25},{2,10},{10,18},{18,26},{... | collective-permute-start | bytes 12296 | tf_op jit(solution)/shard_map/ppermute | solution.py:22
  373.2 4.5 collective-permute-start.23
  374.6 3.1 copy-start.18
  377.7 4.2 copy-start.19
  377.8 5.7 collective-permute-start.24
  381.9 5.5 collective-permute-start.25
  399.0 12.0 %copy-start.20 = (f32[8,128,128]{1,0,2:T(8,128)S(1)}, f32[8,128,128]{1,0,2:T(8,128)}, u32[]{:S(2)}) copy-start(f32[8,128,128]{1,0,2:T(8,128)} %get-tuple-element.198) | copy-start | bytes 1572868
  399.0 201.3 %all-to-all-start.2 = ((f32[32,9,4096]{2,1,0:T(8,128)}), f32[32,9,4096]{2,1,0:T(8,128)}, u32[]{:S(2)}, u32[]{:S(2)}) async-start(f32[32,9,4096]{2,1,0:T(8,128)} %copy.101), calls=%async_computation.2 | async-start | bytes 16777216 | tf_op jit(solution)/shard_map/all_to_all | solution.py:152
  (5 other events, 6.6 us)
where the time goes:
time: 752 us; the launch traced here: 747 us
  waiting for transfers between devices  283 us (38%)
  matrix products  186 us (25%)
  local copies, waits for them, and re-layouts  132 us (18%)
  starting transfers between devices  115 us (15%)
  other arithmetic  28.4 us (4%)
    all_to_all x1, waiting for transfers between devices, on_device(): lax.all_to_all(back_slots.reshape(devices, capacity, width), ('gx', 'gy')...  188 us
    dot_general x24, matrix products, bin_group(): return jnp.einsum('kxc,kyc->kxy', row_hot, col_hot, precision=highest)  111 us
    dot_general x24, matrix products, cell_group(): spread = jnp.einsum('kaxy,kyc->kaxc', slopes, col_hot, precision=highest)  70.6 us
    ppermute x12, starting transfers between devices, with_halo(): before = lax.ppermute(last, axis, up)  65.9 us
    all_to_all x1, waiting for transfers between devices, on_device(): lax.all_to_all(send_maps.reshape(devices, capacity, tile_bins), ('gx', 'g...  65.7 us
    ppermute x12, waiting for transfers between devices, with_halo(): after = lax.ppermute(initial, axis, down)  24.6 us
    eq x24, local copies, waits for them, and re-layouts, cell_group(): rows_in[:, None, :] == row_iota[None, :, None]  21.1 us
    mul x24, local copies, waits for them, and re-layouts, bin_group(): (rows_in[:, None, :] == row_iota[None, :, None]).astype(jnp.float32)  20.4 us
  transfers between devices with their start and end apart: 29, of which 13 were waited for; matrix products, arithmetic and copies ran while one was open for 21% of the time, Pallas kernels for 0%

commit v1 on v0

v1 whole, which is shorter than its diff:
```python
import functools

import jax
import jax.numpy as jnp
from jax import lax
from jax.experimental import pallas as pl
from jax.experimental.pallas import tpu as pltpu
from jax.sharding import PartitionSpec as P

TROWS = 16
GROUP = 8
HALO = 5
PAD_ROWS = 16
VMEM_LIMIT = 48 * 1024 * 1024


def bin_kernel(dest_ref, power_ref, bin_ref, map_ref):
    step = pl.program_id(0)
    cells = power_ref.shape[1]
    cols = map_ref.shape[1]

    @pl.when(step == 0)
    def _():
        map_ref[...] = jnp.zeros_like(map_ref)

    power = power_ref[...]
    bins = bin_ref[...]
    high = power.astype(jnp.bfloat16).astype(jnp.float32)
    low = power - high
    col = lax.bitwise_and(bins, cols - 1)
    row = lax.shift_right_logical(bins, cols.bit_length() - 1)
    col = col.astype(jnp.float32)
    row = row.astype(jnp.float32)
    col_iota = lax.broadcasted_iota(jnp.int32, (cols, cells), 0).astype(jnp.float32).astype(jnp.bfloat16)
    row_iota = lax.broadcasted_iota(jnp.int32, (TROWS, cells), 0).astype(jnp.float32).astype(jnp.bfloat16)
    one = jnp.ones((), jnp.bfloat16)
    zero = jnp.zeros((), jnp.bfloat16)
    for s in range(GROUP):
        def spread(x, n):
            return jnp.broadcast_to(x[s : s + 1, :], (n, cells)).astype(jnp.bfloat16)

        col_hot = jnp.where(spread(col, cols) == col_iota, one, zero)
        row_mask = spread(row, TROWS) == row_iota
        left = jnp.concatenate(
            [
                jnp.where(row_mask, spread(high, TROWS), zero),
                jnp.where(row_mask, spread(low, TROWS), zero),
            ],
            axis=0,
        )
        tile = lax.dot_general(
            left, col_hot, (((1,), (1,)), ((), ())), preferred_element_type=jnp.float32
        )
        start = pl.multiple_of(dest_ref[step * GROUP + s] * TROWS, TROWS)
        map_ref[pl.ds(start, TROWS), :] += tile[:TROWS] + tile[TROWS:]


def bin_cells(dest, cell_power, cell_bin, map_rows, cols):
    blocks, cells = cell_power.shape
    return pl.pallas_call(
        bin_kernel,
        grid_spec=pltpu.PrefetchScalarGridSpec(
            num_scalar_prefetch=1,
            grid=(blocks // GROUP,),
            in_specs=[pl.BlockSpec((GROUP, cells), lambda i, d: (i, 0))] * 2,
            out_specs=pl.BlockSpec((map_rows, cols), lambda i, d: (0, 0)),
        ),
        out_shape=jax.ShapeDtypeStruct((map_rows, cols), jnp.float32),
        compiler_params=pltpu.CompilerParams(vmem_limit_bytes=VMEM_LIMIT),
        cost_estimate=pl.CostEstimate(
            flops=blocks * cells * cols * TROWS * 12, bytes_accessed=40 * 1024 * 1024, transcendentals=0
        ),
        name="bin_cells",
    )(dest, cell_power, cell_bin)


def grad_kernel(size_gx, size_gy, dest_ref, power_ref, bin_ref, sens_ref, out_ref, slope_ref, table_ref):
    step = pl.program_id(0)
    cells = power_ref.shape[1]
    owners, rows, cols = sens_ref.shape

    @pl.when(step == 0)
    def _():
        row_id = lax.broadcasted_iota(jnp.int32, (rows, cols), 0)
        col_id = lax.broadcasted_iota(jnp.int32, (rows, cols), 1)

        def one(o, carry):
            i = o // size_gy
            j = lax.rem(o, size_gy)
            here = sens_ref[o]
            above = sens_ref[jnp.maximum(o - size_gy, 0), rows - 1 :, :]
            below = sens_ref[jnp.minimum(o + size_gy, owners - 1), :1, :]
            above = jnp.where(i > 0, above, 0.0)
            below = jnp.where(i < size_gx - 1, below, 0.0)
            before = pltpu.roll(sens_ref[jnp.maximum(o - 1, 0)], 1, 1)
            after = pltpu.roll(sens_ref[jnp.minimum(o + 1, owners - 1)], cols - 1, 1)
            before = jnp.where(j > 0, before, 0.0)
            after = jnp.where(j < size_gy - 1, after, 0.0)
            down = jnp.where(row_id == rows - 1, below, pltpu.roll(here, rows - 1, 0))
            up = jnp.where(row_id == 0, above, pltpu.roll(here, 1, 0))
            right = jnp.where(col_id == cols - 1, after, pltpu.roll(here, cols - 1, 1))
            left = jnp.where(col_id == 0, before, pltpu.roll(here, 1, 1))
            at = pl.ds(pl.multiple_of(o * rows, rows), rows)
            slope_ref[0, at, :] = 0.5 * (down - up)
            slope_ref[1, at, :] = 0.5 * (right - left)
            return carry

        lax.fori_loop(0, owners, one, 0)

    for s in range(GROUP):
        start = pl.multiple_of(dest_ref[step * GROUP + s] * TROWS, TROWS)
        for a in range(2):
            table_ref[a, :, s, :] = slope_ref[a, pl.ds(start, TROWS), :]
    for c in range(cells // cols):
        at = slice(c * cols, (c + 1) * cols)
        bins = bin_ref[:, at]
        power = power_ref[:, at]
        col = lax.bitwise_and(bins, cols - 1)
        row = lax.shift_right_logical(bins, cols.bit_length() - 1)
        masks = [lax.bitwise_and(row, 1 << b) != 0 for b in range(4)]
        for a in range(2):
            picks = [
                jnp.take_along_axis(table_ref[a, r], col, axis=1, mode="promise_in_bounds")
                for r in range(TROWS)
            ]
            for mask in masks:
                picks = [jnp.where(mask, picks[2 * k + 1], picks[2 * k]) for k in range(len(picks) // 2)]
            out_ref[a, :, at] = picks[0] * power


def cell_grads(dest, cell_power, cell_bin, sens, size_gx, size_gy):
    blocks, cells = cell_power.shape
    owners, rows, cols = sens.shape
    return pl.pallas_call(
        functools.partial(grad_kernel, size_gx, size_gy),
        grid_spec=pltpu.PrefetchScalarGridSpec(
            num_scalar_prefetch=1,
            grid=(blocks // GROUP,),
            in_specs=[pl.BlockSpec((GROUP, cells), lambda i, d: (i, 0))] * 2
            + [pl.BlockSpec((owners, rows, cols), lambda i, d: (0, 0, 0))],
            out_specs=pl.BlockSpec((2, GROUP, cells), lambda i, d: (0, i, 0)),
            scratch_shapes=[
                pltpu.VMEM((2, owners * rows, cols), jnp.float32),
                pltpu.VMEM((2, TROWS, GROUP, cols), jnp.float32),
            ],
        ),
        out_shape=jax.ShapeDtypeStruct((2, blocks, cells), jnp.float32),
        compiler_params=pltpu.CompilerParams(vmem_limit_bytes=VMEM_LIMIT),
        name="cell_grads",
    )(dest, cell_power, cell_bin, sens)


def roll(x, distance, axis):
    return pltpu.roll(x, distance % x.shape[axis], axis)


def sweep_kernel(mask_ref, stack_ref, power_ref, temp_out, sens_out, west_s, south_s, inv_s, a_s, b_s):
    layers = stack_ref.shape[1]
    mask = mask_ref[...]
    for l in range(layers):
        east = stack_ref[1, l]
        north = stack_ref[2, l]
        west = roll(east, 1, 0)
        south = roll(north, 1, 1)
        diag = east + west + north + south + stack_ref[3, l]
        if l:
            diag = diag + stack_ref[3, l - 1]
        west_s[l] = west
        south_s[l] = south
        inv_s[l] = jnp.where(mask > 0.0, 1.0 / diag, 0.0)

    def coupling(field, l):
        v = field(l)
        out = (
            stack_ref[1, l] * roll(v, -1, 0)
            + west_s[l] * roll(v, 1, 0)
            + stack_ref[2, l] * roll(v, -1, 1)
            + south_s[l] * roll(v, 1, 1)
        )
        if l + 1 < layers:
            out = out + stack_ref[3, l] * field(l + 1)
        if l:
            out = out + stack_ref[3, l - 1] * field(l - 1)
        return out

    def sweep(field, out_ref):
        for l in range(layers):
            summed = coupling(field, l)
            if l == 0:
                summed = summed + power_ref[...]
            out_ref[l] = summed * inv_s[l]

    rows, cols = sens_out.shape
    sweep(lambda l: stack_ref[0, l], a_s)
    sweep(lambda l: a_s[l], b_s)
    sweep(lambda l: b_s[l], a_s)
    for l in range(layers):
        temp_out[l] = a_s[l, :rows, :cols]
        b_s[l] = stack_ref[4, l] * a_s[l] * inv_s[l]
    for l in range(2):
        a_s[l] = coupling(lambda k: b_s[k], l) * inv_s[l]
    last = coupling(lambda k: a_s[k], 0) * inv_s[0]
    total = b_s[0] + a_s[0] + last
    sens_out[...] = total[:rows, :cols]


def sweeps(mask, stack, power, rows, cols):
    _, layers, wide_rows, wide_cols = stack.shape
    field = pltpu.VMEM((layers, wide_rows, wide_cols), jnp.float32)
    return pl.pallas_call(
        sweep_kernel,
        out_shape=(
            jax.ShapeDtypeStruct((layers, rows, cols), jnp.float32),
            jax.ShapeDtypeStruct((rows, cols), jnp.float32),
        ),
        in_specs=[pl.BlockSpec(memory_space=pltpu.VMEM)] * 3,
        out_specs=(pl.BlockSpec(memory_space=pltpu.VMEM),) * 2,
        scratch_shapes=[field] * 5,
        compiler_params=pltpu.CompilerParams(vmem_limit_bytes=VMEM_LIMIT),
        name="sweeps",
    )(mask, stack, power)


def padded(array, width, row_dim):
    for axis, dim, room in (("gx", row_dim, PAD_ROWS), ("gy", row_dim + 1, array.shape[row_dim + 1])):
        peers = lax.axis_size(axis)
        length = array.shape[dim] if dim == row_dim else room
        up = [(i, i + 1) for i in range(peers - 1)]
        down = [(j, i) for i, j in up]
        last = lax.slice_in_dim(array, length - width, length, axis=dim)
        first = lax.slice_in_dim(array, 0, width, axis=dim)
        before = lax.ppermute(last, axis, up)
        after = lax.ppermute(first, axis, down)
        shape = list(array.shape)
        shape[dim] = room - 2 * width
        gap = jnp.zeros(shape, array.dtype)
        array = jnp.concatenate([array, after, gap, before], axis=dim)
    return array


def inside_mask(rows, cols):
    def axis_ok(axis, length, room):
        place = lax.broadcasted_iota(jnp.int32, (length + room,), 0)
        offset = jnp.where(place >= length + room // 2, place - (length + room), place)
        near = (offset >= -(HALO - 1)) & (offset < length + HALO - 1)
        whole = lax.axis_index(axis) * length + offset
        return near & (whole >= 0) & (whole < length * lax.axis_size(axis))

    ok = axis_ok("gx", rows, PAD_ROWS)[:, None] & axis_ok("gy", cols, cols)[None, :]
    return ok.astype(jnp.float32)


def on_device(
    cell_power, cell_bin, block_owner, block_tile, temp_prev, cond_x, cond_y, cond_z, weight
):
    _, rows, cols = temp_prev.shape
    tiles = rows // TROWS
    size_gx, size_gy = lax.axis_size("gx"), lax.axis_size("gy")
    devices = size_gx * size_gy
    dest = block_owner[:, 0] * tiles + block_tile
    stack = padded(jnp.stack([temp_prev, cond_x, cond_y, cond_z, weight]), HALO, 2)
    mask = inside_mask(rows, cols)
    partial = bin_cells(dest, cell_power, cell_bin, devices * rows, cols)
    power_map = lax.psum_scatter(partial, ("gx", "gy"), scatter_dimension=0, tiled=True)
    power_map = padded(power_map, HALO - 1, 0)
    temperature, sensitivity = sweeps(mask, stack, power_map, rows, cols)
    sens = lax.all_gather(sensitivity, ("gx", "gy"), axis=0, tiled=False)
    grads = cell_grads(dest, cell_power, cell_bin, sens, size_gx, size_gy)
    return temperature, grads


def solution(mesh):
    cells = P(("gx", "gy"), None)
    grid = P(None, "gx", "gy")
    return jax.shard_map(
        on_device,
        mesh=mesh,
        in_specs=(cells, cells, cells, P(("gx", "gy")), grid, grid, grid, grid, grid),
        out_specs=(grid, P(None, ("gx", "gy"), None)),
        check_vma=False,
    )
```

time: 752 us -> 310 us (0.41)
  matrix products: 186 us -> 0 us
  waiting for transfers between devices: 283 us -> 176 us
  local copies, waits for them, and re-layouts: 132 us -> 27.6 us
  starting transfers between devices: 115 us -> 14.3 us
  Pallas kernels: 0 us -> 69.9 us
  other arithmetic: 28.4 us -> 6.96 us
  between operations: 1.45 us -> 14.2 us
    all_to_all x3 -> x0, waiting for transfers between devices: 254 us -> none  [the longest x1 188 us: on_device(): lax.all_to_all(back_slots.reshape(devices, capacity, width), ('gx', 'gy')...]
    dot_general x50 -> x0, matrix products: 186 us -> none  [the longest x24 111 us: bin_group(): return jnp.einsum('kxc,kyc->kxy', row_hot, col_hot, precision=highest)]
    reduce_scatter x0 -> x1, waiting for transfers between devices: none -> 113 us  [on_device(): lax.psum_scatter(partial, ('gx', 'gy'), scatter_dimension=0, tiled=True)]
    ppermute x26 -> x8, starting transfers between devices: 89.2 us -> 14.2 us  [the longest x4 9.03 us: padded(): before = lax.ppermute(last, axis, up)]
    pallas_call x0 -> x3, Pallas kernels: none -> 69.9 us  [the longest x1 39.5 us: bin_cells(): pl.pallas_call(bin_kernel, grid_spec=pltpu.PrefetchScalarGridSpec(num_sca...]
    all_gather x0 -> x1, waiting for transfers between devices: none -> 58.7 us  [on_device(): sens = lax.all_gather(sensitivity, ('gx', 'gy'), axis=0, tiled=False)]
    mul x50 -> x0, local copies, waits for them, and re-layouts: 41 us -> none  [the longest x24 20.4 us: bin_group(): (rows_in[:, None, :] == row_iota[None, :, None]).astype(jnp.float32)]
    all_to_all x3 -> x0, starting transfers between devices: 25.3 us -> none  [the longest x1 12 us: on_device(): lax.all_to_all(back_slots.reshape(devices, capacity, width), ('gx', 'gy')...]
  transfers between devices with their start and end apart: 29 -> 10, of which waited for: 13 -> 4; matrix products, arithmetic and copies ran while one was open for 21% -> 9% of each run, Pallas kernels for 0% -> 0%
where the time goes in v1:
time: 310 us; the launch traced here: 309 us
  waiting for transfers between devices  176 us (57%)
  Pallas kernels  69.9 us (23%)
  local copies, waits for them, and re-layouts  27.6 us (9%)
  starting transfers between devices  14.3 us (5%)
  between operations  14.2 us (5%)
  other arithmetic  6.96 us (2%)
    reduce_scatter x1, waiting for transfers between devices, on_device(): lax.psum_scatter(partial, ('gx', 'gy'), scatter_dimension=0, tiled=True)  113 us
    all_gather x1, waiting for transfers between devices, on_device(): sens = lax.all_gather(sensitivity, ('gx', 'gy'), axis=0, tiled=False)  58.7 us
    pallas_call x1, Pallas kernels, bin_cells(): pl.pallas_call(bin_kernel, grid_spec=pltpu.PrefetchScalarGridSpec(num_sca...  39.5 us
    pallas_call x1, Pallas kernels, cell_grads(): pl.pallas_call(functools.partial(grad_kernel, size_gx, size_gy), grid_spe...  23.6 us
    ppermute x4, starting transfers between devices, padded(): before = lax.ppermute(last, axis, up)  9.03 us
    slice x5, local copies, waits for them, and re-layouts, padded(): first = lax.slice_in_dim(array, 0, width, axis=dim)  8.29 us
    unnamed x18, local copies, waits for them, and re-layouts  7.7 us
    pallas_call x1, Pallas kernels, sweeps(): pl.pallas_call(sweep_kernel, out_shape=(jax.ShapeDtypeStruct((layers, row...  6.77 us
  transfers between devices with their start and end apart: 10, of which 4 were waited for; matrix products, arithmetic and copies ran while one was open for 9% of the time, Pallas kernels for 0%

profile of v1, /device:TPU:0, one launch (start us, length us, event | category | flops | bytes accessed | tf_op | source)
XLA Modules:
  0.0 309.3 jit_solution(14847584826458918693)
XLA Ops:
  7.2 0.0 reduce-scatter.2.cloned.1.call-start
  7.2 0.7 broadcast_multiply_fusion
  7.9 0.7 add.39.dest_ref
  8.6 1.4 copy-done.1
  10.0 1.4 copy-done.3
  11.4 39.5 %bin_cells.1 = f32[4096,128]{1,0:T(8,128)} custom-call(s32[192]{0:T(256)S(1)} %add.39.dest_ref, f32[192,2048]{1,0:T(8,128)S(1)} %copy-done.1, s32[192,2048]{1,0:T(8,128)S(1)} %copy-done.3), custom_call_target="tpu_custom_call" | custom-call | flops 9663676416 | bytes 41943040 | tf_op jit(solution)/shard_map/bin_cells/pallas_call | solution.py:60
  50.9 0.0 reduce-scatter.2.cloned.1.call-update
  50.9 0.0 all-gather.3.cloned.1.call-start
  51.0 1.1 bitcast_dynamic-update-slice_fusion.3
  52.1 1.1 bitcast_dynamic-update-slice_fusion.2
  53.2 1.1 bitcast_dynamic-update-slice_fusion.1
  54.3 1.1 bitcast_dynamic-update-slice_fusion
  55.4 2.4 collective-permute-start.1
  57.8 1.3 collective-permute-start
  59.1 0.0 collective-permute-done.1
  59.1 4.0 %collective-permute-done = f32[5,8,5,128]{3,2,1,0:T(8,128)S(1)} collective-permute-done((f32[5,8,5,128]{3,2,1,0:T(8,128)S(1)}, f32[5,8,5,128]{3,2,1,0:T(8,128)S(1)}, u32[]{:S(2)}, u32[]{:S(2)}) %collective-permute-start) | collective-permute-done | bytes 102432 | tf_op jit(solution)/shard_map/ppermute | solution.py:233
  63.2 0.2 pad_maximum_fusion.1
  63.4 3.5 %fusion = (f32[5,8,144,5]{3,2,1,0:T(8,128)}, f32[5,8,144,5]{3,2,1,0:T(8,128)}) fusion(f32[5,8,144,128]{3,2,1,0:T(8,128)S(1)} %pad_maximum_fusion.1), kind=kLoop, calls=%fused_computation.15 | loop fusion | bytes 460800 | tf_op jit(solution)/shard_map/slice | solution.py:231
  67.0 4.0 %copy.12 = f32[5,8,144,5]{2,1,3,0:T(8,128)} copy(f32[5,8,144,5]{3,2,1,0:T(8,128)} %get-tuple-element.7) | data formatting | bytes 230400 | tf_op jit(solution)/shard_map/slice | solution.py:230
  70.9 4.1 %collective-permute-start.3 = (f32[5,8,144,5]{2,1,3,0:T(8,128)}, f32[5,8,144,5]{2,1,3,0:T(8,128)}, u32[]{:S(2)}, u32[]{:S(2)}) collective-permute-start(f32[5,8,144,5]{2,1,3,0:T(8,128)} %copy.12), channel_id=1, source_target_pairs={{0,1},{1,2},{2,3},{3,4},{4,5},{5,6},{6,7},{8,9},{9,10},{10,11},{11... | collective-permute-start | bytes 345608 | tf_op jit(solution)/shard_map/ppermute | solution.py:232
  75.0 3.9 %copy.11 = f32[5,8,144,5]{2,1,3,0:T(8,128)} copy(f32[5,8,144,5]{3,2,1,0:T(8,128)} %get-tuple-element.6) | data formatting | bytes 230400 | tf_op jit(solution)/shard_map/slice | solution.py:231
  79.0 1.3 collective-permute-start.2
  80.3 113.0 %reduce-scatter.2.cloned.1.call-done = f32[128,128]{1,0:T(8,128)} async-done(((f32[4096,128]{1,0:T(8,128)}), f32[128,128]{1,0:T(8,128)}) %reduce-scatter.2.cloned.1.call-update) | async-done | bytes 65552 | tf_op jit(solution)/shard_map/reduce_scatter | solution.py:264
  193.3 0.7 fusion.3
  194.0 1.3 collective-permute-start.5
  195.3 1.3 collective-permute-start.4
  196.6 0.1 and_convert_fusion.mask_ref
  196.7 0.1 pad.16.clone
  196.7 0.1 pad.5.clone
  196.8 0.0 collective-permute-done.3
  196.8 3.2 %copy.14 = f32[5,8,144,5]{3,2,1,0:T(8,128)} copy(f32[5,8,144,5]{2,1,3,0:T(8,128)} %collective-permute-done.3) | data formatting | bytes 230400 | tf_op jit(solution)/shard_map/ppermute | solution.py:232
  200.0 0.0 collective-permute-done.2
  200.0 3.2 %copy.13 = f32[5,8,144,5]{3,2,1,0:T(8,128)} copy(f32[5,8,144,5]{2,1,3,0:T(8,128)} %collective-permute-done.2) | data formatting | bytes 230400 | tf_op jit(solution)/shard_map/ppermute | solution.py:233
  203.3 0.0 collective-permute-done.5
  203.3 0.0 collective-permute-done.4
  203.3 0.1 fusion.2
  203.4 1.3 collective-permute-start.7
  204.7 1.3 collective-permute-start.6
  206.0 5.1 %pad_maximum_fusion.stack_ref = f32[5,8,144,256]{3,2,1,0:T(8,128)} fusion(f32[5,8,144,5]{3,2,1,0:T(8,128)} %copy.14, f32[5,8,144,5]{3,2,1,0:T(8,128)} %copy.13, f32[5,8,5,128]{3,2,1,0:T(8,128)S(1)} %collective-permute-done.1, f32[5,8,6,128]{3,2,1,0:T(8,128)S(1)} %broadcast_in_dim.14, f32[5,8,5,128]{3,2,1,0:T(8,128)S(1)} %collective-permute-done, ...), kind=kLoop, calls=%fused_computation | loop fusion | flops 8847360 | bytes 9078784 | tf_op jit(solution)/shard_map/concatenate | solution.py:237
  211.1 0.4 collective-permute-done.6
  211.6 0.1 pad_maximum_fusion.2.power_ref
  211.7 0.0 copy-start.2
  211.7 0.0 copy-start.4
  211.7 6.8 %sweeps.1 = (f32[8,128,128]{2,1,0:T(8,128)}, f32[128,128]{1,0:T(8,128)}) custom-call(f32[144,256]{1,0:T(8,128)S(1)} %and_convert_fusion.mask_ref, f32[5,8,144,256]{3,2,1,0:T(8,128)} %pad_maximum_fusion.stack_ref, f32[144,256]{1,0:T(8,128)S(1)} %pad_maximum_fusion.2.power_ref), custom_call_target="tpu_custom_call" | custom-call | tf_op jit(solution)/shard_map/sweeps/pallas_call | solution.py:210
  218.5 0.0 all-gather.3.cloned.1.call-update
  218.5 58.7 %all-gather.3.cloned.1.call-done = f32[4096,128]{1,0:T(8,128)} async-done(((f32[128,128]{1,0:T(8,128)}), f32[4096,128]{1,0:T(8,128)}) %all-gather.3.cloned.1.call-update) | async-done | bytes 2097168 | tf_op jit(solution)/shard_map/all_gather | solution.py:267
  277.2 1.6 copy-done
  278.8 23.6 %cell_grads.1 = f32[2,192,2048]{2,1,0:T(8,128)} custom-call(s32[192]{0:T(256)S(1)} %add.39.dest_ref, f32[192,2048]{1,0:T(8,128)S(1)} %copy-done.2, s32[192,2048]{1,0:T(8,128)S(1)} %copy-done.4, f32[32,128,128]{2,1,0:T(8,128)S(1)} %bitcast.12), custom_call_target="tpu_custom_call" | custom-call | tf_op jit(solution)/shard_map/cell_grads/pallas_call | solution.py:134
  (19 shorter events, 0.1 us)
Async XLA Ops:
  7.2 186.1 %reduce-scatter.2.cloned.1.call-start = ((), (), s32[]{:S(2)}) async-start(), calls=%async_computation.1 | async-start | bytes 2162688 | tf_op jit(solution)/shard_map/reduce_scatter | solution.py:264
  8.6 1.4 copy-start.1
  10.0 1.4 copy-start.3
  11.4 39.6 %copy-start.5 = (f32[8,128,128]{2,1,0:T(8,128)S(1)}, f32[8,128,128]{2,1,0:T(8,128)}, u32[]{:S(2)}) copy-start(f32[8,128,128]{2,1,0:T(8,128)} %param.13) | copy-start | bytes 1572868
  50.9 226.3 %all-gather.3.cloned.1.call-start = ((), (), s32[]{:S(2)}) async-start(), calls=%async_computation.2 | async-start | bytes 2162688 | tf_op jit(solution)/shard_map/all_gather | solution.py:267
  55.4 3.7 %collective-permute-start.1 = (f32[5,8,5,128]{3,2,1,0:T(8,128)S(1)}, f32[5,8,5,128]{3,2,1,0:T(8,128)S(1)}, u32[]{:S(2)}, u32[]{:S(2)}) collective-permute-start(f32[5,8,5,128]{3,2,1,0:T(8,128)S(1)} %get-tuple-element.9), channel_id=1, source_target_pairs={{0,8},{8,16},{16,24},{1,9},{9,17},{17,25},{2,10},{10,18},{18,26},{... | collective-permute-start | bytes 307208 | tf_op jit(solution)/shard_map/ppermute | solution.py:232
  57.8 5.4 %collective-permute-start = (f32[5,8,5,128]{3,2,1,0:T(8,128)S(1)}, f32[5,8,5,128]{3,2,1,0:T(8,128)S(1)}, u32[]{:S(2)}, u32[]{:S(2)}) collective-permute-start(f32[5,8,5,128]{3,2,1,0:T(8,128)S(1)} %get-tuple-element.8), channel_id=1, source_target_pairs={{8,0},{16,8},{24,16},{9,1},{17,9},{25,17},{10,2},{18,10},{26,18},{... | collective-permute-start | bytes 307208 | tf_op jit(solution)/shard_map/ppermute | solution.py:233
  70.9 125.9 %collective-permute-start.3 = (f32[5,8,144,5]{2,1,3,0:T(8,128)}, f32[5,8,144,5]{2,1,3,0:T(8,128)}, u32[]{:S(2)}, u32[]{:S(2)}) collective-permute-start(f32[5,8,144,5]{2,1,3,0:T(8,128)} %copy.12), channel_id=1, source_target_pairs={{0,1},{1,2},{2,3},{3,4},{4,5},{5,6},{6,7},{8,9},{9,10},{10,11},{11... | collective-permute-start | bytes 345608 | tf_op jit(solution)/shard_map/ppermute | solution.py:232
  79.0 121.0 %collective-permute-start.2 = (f32[5,8,144,5]{2,1,3,0:T(8,128)}, f32[5,8,144,5]{2,1,3,0:T(8,128)}, u32[]{:S(2)}, u32[]{:S(2)}) collective-permute-start(f32[5,8,144,5]{2,1,3,0:T(8,128)} %copy.11), channel_id=1, source_target_pairs={{1,0},{2,1},{3,2},{4,3},{5,4},{6,5},{7,6},{9,8},{10,9},{11,10},{12... | collective-permute-start | bytes 345608 | tf_op jit(solution)/shard_map/ppermute | solution.py:233
  194.0 9.3 %collective-permute-start.5 = (f32[4,128]{1,0:T(4,128)S(1)}, f32[4,128]{1,0:T(4,128)S(1)}, u32[]{:S(2)}, u32[]{:S(2)}) collective-permute-start(f32[4,128]{1,0:T(4,128)S(1)} %get-tuple-element.13), channel_id=1, source_target_pairs={{0,8},{8,16},{16,24},{1,9},{9,17},{17,25},{2,10},{10,18},{18,26},{... | collective-permute-start | bytes 6152 | tf_op jit(solution)/shard_map/ppermute | solution.py:232
  195.3 8.0 %collective-permute-start.4 = (f32[4,128]{1,0:T(4,128)S(1)}, f32[4,128]{1,0:T(4,128)S(1)}, u32[]{:S(2)}, u32[]{:S(2)}) collective-permute-start(f32[4,128]{1,0:T(4,128)S(1)} %get-tuple-element.12), channel_id=1, source_target_pairs={{8,0},{16,8},{24,16},{9,1},{17,9},{25,17},{10,2},{18,10},{26,18},{... | collective-permute-start | bytes 6152 | tf_op jit(solution)/shard_map/ppermute | solution.py:233
  196.8 6.5 %copy-start.6 = (f32[128,128]{1,0:T(8,128)S(1)}, f32[128,128]{1,0:T(8,128)}, u32[]{:S(2)}) copy-start(f32[128,128]{1,0:T(8,128)} %reduce-scatter.2.cloned.1.call-done) | copy-start | bytes 196612
  203.4 7.7 %collective-permute-start.7 = (f32[144,4]{1,0:T(8,128)S(1)}, f32[144,4]{1,0:T(8,128)S(1)}, u32[]{:S(2)}, u32[]{:S(2)}) collective-permute-start(f32[144,4]{1,0:T(8,128)S(1)} %get-tuple-element.11), channel_id=1, source_target_pairs={{0,1},{1,2},{2,3},{3,4},{4,5},{5,6},{6,7},{8,9},{9,10},{10,11},{11... | collective-permute-start | bytes 6920 | tf_op jit(solution)/shard_map/ppermute | solution.py:232
  204.7 6.9 %collective-permute-start.6 = (f32[144,4]{1,0:T(8,128)S(1)}, f32[144,4]{1,0:T(8,128)S(1)}, u32[]{:S(2)}, u32[]{:S(2)}) collective-permute-start(f32[144,4]{1,0:T(8,128)S(1)} %get-tuple-element.10), channel_id=1, source_target_pairs={{1,0},{2,1},{3,2},{4,3},{5,4},{6,5},{7,6},{9,8},{10,9},{11,10},{12... | collective-permute-start | bytes 6920 | tf_op jit(solution)/shard_map/ppermute | solution.py:233
  211.7 65.6 %copy-start.2 = (f32[192,2048]{1,0:T(8,128)S(1)}, f32[192,2048]{1,0:T(8,128)}, u32[]{:S(2)}) copy-start(f32[192,2048]{1,0:T(8,128)} %power_ref.3) | copy-start | bytes 4718596
  211.7 65.5 %copy-start.4 = (s32[192,2048]{1,0:T(8,128)S(1)}, s32[192,2048]{1,0:T(8,128)}, u32[]{:S(2)}) copy-start(s32[192,2048]{1,0:T(8,128)} %bin_ref.3) | copy-start | bytes 4718596
  277.2 1.6 copy-start
Sparse Core Ops, SparseCore 0:
  51.0 142.1 reduce-scatter.1
  218.6 58.5 all-gather.2

commit v2 on v1

--- a/solution.py
+++ b/solution.py
@@ -154,8 +154,106 @@
     return pltpu.roll(x, distance % x.shape[axis], axis)
 
 
-def sweep_kernel(mask_ref, stack_ref, power_ref, temp_out, sens_out, west_s, south_s, inv_s, a_s, b_s):
+def remote(src, dst, sems, at, device):
+    return pltpu.make_async_remote_copy(
+        src_ref=src,
+        dst_ref=dst,
+        send_sem=sems.at[(0, *at)],
+        recv_sem=sems.at[(1, *at)],
+        device_id=device,
+        device_id_type=pl.DeviceIdType.MESH,
+    )
+
+
+def sweep_kernel(
+    size_gx,
+    size_gy,
+    mask_ref,
+    stack_ref,
+    partial_ref,
+    temp_out,
+    sens_out,
+    west_s,
+    south_s,
+    inv_s,
+    a_s,
+    b_s,
+    core_buf,
+    x_buf,
+    x_sum,
+    y_buf,
+    wide,
+    sides,
+    power_s,
+    sens,
+    core_sems,
+    x_sems,
+    y_sems,
+    halo_sems,
+    back_y,
+    back_x,
+    back_core,
+):
     layers = stack_ref.shape[1]
+    _, rows, cols = partial_ref.shape
+    size_x = size_gx // 2
+    gx, gy = lax.axis_index("gx"), lax.axis_index("gy")
+    x, core = gx // 2, lax.rem(gx, 2)
+    partner = (x * 2 + 1 - core, gy)
+
+    def ahead(dj):
+        return lax.rem(gy + dj, size_gy)
+
+    def behind(dj):
+        return lax.rem(gy + size_gy - dj, size_gy)
+
+    def x_ahead(d):
+        return lax.rem(x + d, size_x)
+
+    def x_behind(d):
+        return lax.rem(x + size_x - d, size_x)
+
+    barrier = pltpu.get_barrier_semaphore()
+    for d in range(1, size_gx):
+        pl.semaphore_signal(
+            barrier,
+            inc=1,
+            device_id=(lax.rem(gx + d, size_gx), gy),
+            device_id_type=pl.DeviceIdType.MESH,
+        )
+    for d in range(1, size_gy):
+        pl.semaphore_signal(
+            barrier, inc=1, device_id=(gx, ahead(d)), device_id_type=pl.DeviceIdType.MESH
+        )
+    pl.semaphore_wait(barrier, size_gx + size_gy - 2)
+
+    def to_core(dj, t):
+        src = partial_ref.at[(t * 2 + 1 - core) * size_gy + ahead(dj)]
+        return remote(src, core_buf.at[t, dj], core_sems, (t, dj), partner)
+
+    def to_x(dj, d):
+        src = core_buf.at[x_ahead(d), dj]
+        return remote(src, x_buf.at[d - 1, dj], x_sems, (d - 1, dj), (x_ahead(d) * 2 + core, gy))
+
+    def to_y(dj):
+        return remote(x_sum.at[dj], y_buf.at[dj - 1], y_sems, (dj - 1,), (gx, ahead(dj)))
+
+    def chunk(k):
+        return lax.rem(k + 1, size_gy)
+
+    def loop(count, body, start=0):
+        def wrapped(k, carry):
+            body(k)
+            return carry
+
+        lax.fori_loop(start, count, wrapped, 0)
+
+    def send_core(k):
+        for t in range(size_x):
+            to_core(chunk(k), t).start()
+
+    loop(size_gy, send_core)
+
     mask = mask_ref[...]
     for l in range(layers):
         east = stack_ref[1, l]
@@ -168,6 +266,58 @@
         west_s[l] = west
         south_s[l] = south
         inv_s[l] = jnp.where(mask > 0.0, 1.0 / diag, 0.0)
+
+    def send_x(k):
+        dj = chunk(k)
+        for t in range(size_x):
+            to_core(dj, t).wait_recv()
+            core_buf[t, dj] += partial_ref[(t * 2 + core) * size_gy + ahead(dj)]
+        for d in range(1, size_x):
+            to_x(dj, d).start()
+
+    loop(size_gy, send_x)
+
+    def add_x(dj):
+        total = core_buf[x, dj]
+        for d in range(1, size_x):
+            to_x(dj, d).wait_recv()
+            total = total + x_buf[d - 1, dj]
+        x_sum[dj] = total
+
+    def send_y(dj):
+        add_x(dj)
+        to_y(dj).start()
+
+    loop(size_gy, send_y, 1)
+    add_x(0)
+    wide[:rows] = x_sum[0]
+
+    def add_y(dj):
+        to_y(dj).wait_recv()
+        wide[:rows] += y_buf[dj - 1]
+
+    loop(size_gy, add_y, 1)
+
+    up, down = lax.rem(gx + 1, size_gx), lax.rem(gx + size_gx - 1, size_gx)
+    halo_rows = (
+        remote(wide.at[pl.ds(rows - 8, 8)], wide.at[pl.ds(rows + 8, 8)], halo_sems, (0,), (up, gy)),
+        remote(wide.at[pl.ds(0, 8)], wide.at[pl.ds(rows, 8)], halo_sems, (1,), (down, gy)),
+    )
+    for copy in halo_rows:
+        copy.start()
+    for copy in halo_rows:
+        copy.wait()
+    halo_cols = (
+        remote(wide, sides.at[0], halo_sems, (2,), (gx, ahead(1))),
+        remote(wide, sides.at[1], halo_sems, (3,), (gx, behind(1))),
+    )
+    for copy in halo_cols:
+        copy.start()
+    for copy in halo_cols:
+        copy.wait()
+    lane = lax.broadcasted_iota(jnp.int32, wide.shape, 1)
+    power_s[:, :cols] = wide[...]
+    power_s[:, cols:] = jnp.where(lane < cols // 2, sides[1], sides[0])
 
     def coupling(field, l):
         v = field(l)
@@ -187,10 +337,9 @@
         for l in range(layers):
             summed = coupling(field, l)
             if l == 0:
-                summed = summed + power_ref[...]
+                summed = summed + power_s[...]
             out_ref[l] = summed * inv_s[l]
 
-    rows, cols = sens_out.shape
     sweep(lambda l: stack_ref[0, l], a_s)
     sweep(lambda l: a_s[l], b_s)
     sweep(lambda l: b_s[l], a_s)
@@ -201,24 +350,103 @@
         a_s[l] = coupling(lambda k: b_s[k], l) * inv_s[l]
     last = coupling(lambda k: a_s[k], 0) * inv_s[0]
     total = b_s[0] + a_s[0] + last
-    sens_out[...] = total[:rows, :cols]
-
-
-def sweeps(mask, stack, power, rows, cols):
+    sens[gx * size_gy + gy] = total[:rows, :cols]
+
+    def give_y(dj):
+        mine = sens.at[gx * size_gy + gy]
+        return remote(mine, mine, back_y, (dj - 1,), (gx, ahead(dj)))
+
+    def give_x(dj, d):
+        block = sens.at[gx * size_gy + behind(dj)]
+        return remote(block, block, back_x, (d - 1, dj), (x_ahead(d) * 2 + core, gy))
+
+    def give_core(dj, d):
+        block = sens.at[(x_behind(d) * 2 + core) * size_gy + behind(dj)]
+        return remote(block, block, back_core, (d, dj), partner)
+
+    def pass_on(dj):
+        for d in range(1, size_x):
+            give_x(dj, d).start()
+        give_core(dj, 0).start()
+
+    def receive_y(dj):
+        give_y(dj).wait_recv()
+        pass_on(dj)
+
+    def receive_x(dj):
+        for d in range(1, size_x):
+            give_x(dj, d).wait_recv()
+            give_core(dj, d).start()
+
+    def finish(dj):
+        for d in range(size_x):
+            give_core(dj, d).wait_recv()
+            give_core(dj, d).wait_send()
+            to_core(dj, d).wait_send()
+        for d in range(1, size_x):
+            give_x(dj, d).wait_send()
+            to_x(dj, d).wait_send()
+
+    def finish_y(dj):
+        give_y(dj).wait_send()
+        to_y(dj).wait_send()
+
+    loop(size_gy, lambda dj: give_y(dj).start(), 1)
+    pass_on(0)
+    loop(size_gy, receive_y, 1)
+    loop(size_gy, receive_x)
+    loop(size_gy, finish)
+    loop(size_gy, finish_y, 1)
+
+    def store(o):
+        sens_out[o] = sens[o]
+
+    loop(size_gx * size_gy, store)
+
+
+def sweeps(mask, stack, partial, size_gx, size_gy):
+    owners, rows, cols = partial.shape
     _, layers, wide_rows, wide_cols = stack.shape
-    field = pltpu.VMEM((layers, wide_rows, wide_cols), jnp.float32)
+    size_x = size_gx // 2
+    vmem = pl.BlockSpec(memory_space=pltpu.VMEM)
+
+    def blocks(*lead, length=rows):
+        return pltpu.VMEM((*lead, length, cols), jnp.float32)
+
+    def sems(*shape):
+        return pltpu.SemaphoreType.DMA((2, *shape))
+
     return pl.pallas_call(
-        sweep_kernel,
+        functools.partial(sweep_kernel, size_gx, size_gy),
         out_shape=(
             jax.ShapeDtypeStruct((layers, rows, cols), jnp.float32),
-            jax.ShapeDtypeStruct((rows, cols), jnp.float32),
+            jax.ShapeDtypeStruct((owners, rows, cols), jnp.float32),
         ),
-        in_specs=[pl.BlockSpec(memory_space=pltpu.VMEM)] * 3,
-        out_specs=(pl.BlockSpec(memory_space=pltpu.VMEM),) * 2,
-        scratch_shapes=[field] * 5,
-        compiler_params=pltpu.CompilerParams(vmem_limit_bytes=VMEM_LIMIT),
+        in_specs=[vmem] * 3,
+        out_specs=(vmem, vmem),
+        scratch_shapes=[pltpu.VMEM((layers, wide_rows, wide_cols), jnp.float32)] * 5
+        + [
+            blocks(size_x, size_gy),
+            blocks(size_x - 1, size_gy),
+            blocks(size_gy),
+            blocks(size_gy - 1),
+            blocks(length=wide_rows),
+            blocks(2, length=wide_rows),
+            pltpu.VMEM((wide_rows, wide_cols), jnp.float32),
+            blocks(owners),
+            sems(size_x, size_gy),
+            sems(size_x - 1, size_gy),
+            sems(size_gy - 1),
+            sems(4),
+            sems(size_gy - 1),
+            sems(size_x - 1, size_gy),
+            sems(size_x, size_gy),
+        ],
+        compiler_params=pltpu.CompilerParams(
+            vmem_limit_bytes=56 * 1024 * 1024, collective_id=0, has_side_effects=True
+        ),
         name="sweeps",
-    )(mask, stack, power)
+    )(mask, stack, partial)
 
 
 def padded(array, width, row_dim):
@@ -261,10 +489,8 @@
     stack = padded(jnp.stack([temp_prev, cond_x, cond_y, cond_z, weight]), HALO, 2)
     mask = inside_mask(rows, cols)
     partial = bin_cells(dest, cell_power, cell_bin, devices * rows, cols)
-    power_map = lax.psum_scatter(partial, ("gx", "gy"), scatter_dimension=0, tiled=True)
-    power_map = padded(power_map, HALO - 1, 0)
-    temperature, sensitivity = sweeps(mask, stack, power_map, rows, cols)
-    sens = lax.all_gather(sensitivity, ("gx", "gy"), axis=0, tiled=False)
+    partial = partial.reshape(devices, rows, cols)
+    temperature, sens = sweeps(mask, stack, partial, size_gx, size_gy)
     grads = cell_grads(dest, cell_power, cell_bin, sens, size_gx, size_gy)
     return temperature, grads
 

time: 310 us -> 170 us (0.55)
  waiting for transfers between devices: 176 us -> 0.81 us
  Pallas kernels: 69.9 us -> 119 us
  between operations: 14.2 us -> 0.86 us
    reduce_scatter x1 -> x0, waiting for transfers between devices: 113 us -> none  [on_device(): lax.psum_scatter(partial, ('gx', 'gy'), scatter_dimension=0, tiled=True)]
    all_gather x1 -> x0, waiting for transfers between devices: 58.7 us -> none  [on_device(): sens = lax.all_gather(sensitivity, ('gx', 'gy'), axis=0, tiled=False)]
    pallas_call x1, Pallas kernels: 6.77 us -> 57.2 us  [sweeps(): pl.pallas_call(functools.partial(sweep_kernel, size_gx, size_gy), out_sha...]
    ppermute x4 -> x2, waiting for transfers between devices: 4.48 us -> 0.01 us  [padded(): after = lax.ppermute(first, axis, down)]
    concatenate x4 -> x2, other arithmetic: 5.49 us -> 7.28 us  [padded(): array = jnp.concatenate([array, after, gap, before], axis=dim)]
    ppermute x4 -> x2, starting transfers between devices: 9.03 us -> 9.87 us  [padded(): before = lax.ppermute(last, axis, up)]
    unnamed x18 -> x27, local copies, waits for them, and re-layouts: 7.7 us -> 7.46 us
    slice x5 -> x3, local copies, waits for them, and re-layouts: 8.29 us -> 8.2 us  [padded(): first = lax.slice_in_dim(array, 0, width, axis=dim)]
  transfers between devices with their start and end apart: 10 -> 4, of which waited for: 4 -> 1; matrix products, arithmetic and copies ran while one was open for 9% -> 5% of each run, Pallas kernels for 0% -> 23%
where the time goes in v2:
time: 170 us; the launch traced here: 167 us
  Pallas kernels  119 us (70%)
  local copies, waits for them, and re-layouts  26.2 us (15%)
  starting transfers between devices  12.4 us (7%)
  other arithmetic  8.05 us (5%)
    pallas_call x1, Pallas kernels, sweeps(): pl.pallas_call(functools.partial(sweep_kernel, size_gx, size_gy), out_sha...  57.2 us
    pallas_call x1, Pallas kernels, bin_cells(): pl.pallas_call(bin_kernel, grid_spec=pltpu.PrefetchScalarGridSpec(num_sca...  38.1 us
    pallas_call x1, Pallas kernels, cell_grads(): pl.pallas_call(functools.partial(grad_kernel, size_gx, size_gy), grid_spe...  23.6 us
    ppermute x2, starting transfers between devices, padded(): before = lax.ppermute(last, axis, up)  9.87 us
    slice x3, local copies, waits for them, and re-layouts, padded(): first = lax.slice_in_dim(array, 0, width, axis=dim)  8.2 us
    unnamed x27, local copies, waits for them, and re-layouts  7.46 us
    concatenate x2, other arithmetic, padded(): array = jnp.concatenate([array, after, gap, before], axis=dim)  7.28 us
    slice x1, local copies, waits for them, and re-layouts, padded(): last = lax.slice_in_dim(array, length - width, length, axis=dim)  3.96 us
  transfers between devices with their start and end apart: 4, of which 1 were waited for; matrix products, arithmetic and copies ran while one was open for 5% of the time, Pallas kernels for 23%

profile of v2, /device:TPU:0, one launch (start us, length us, event | category | flops | bytes accessed | tf_op | source)
XLA Modules:
  0.0 167.3 jit_solution(4675641104619295421)
XLA Ops:
  0.6 0.0 copy-start.6
  0.6 0.0 copy-start.7
  0.7 0.0 copy-start.10
  0.7 0.0 copy-start.9
  0.7 0.0 copy-start.3
  0.7 0.0 copy-start.2
  0.7 1.2 bitcast_dynamic-update-slice_fusion.4
  1.9 1.2 bitcast_dynamic-update-slice_fusion.3
  3.2 1.1 bitcast_dynamic-update-slice_fusion.2
  4.2 0.0 copy-done.6
  4.3 0.0 copy-done.7
  4.4 0.0 copy-start.4
  4.4 1.5 copy-done.4
  5.8 0.7 fusion.1
  6.5 1.3 collective-permute-start
  7.8 3.7 %collective-permute-start.1 = (f32[5,8,5,128]{3,2,1,0:T(8,128)S(1)}, f32[5,8,5,128]{3,2,1,0:T(8,128)}, u32[]{:S(2)}, u32[]{:S(2)}) collective-permute-start(f32[5,8,5,128]{3,2,1,0:T(8,128)S(1)} %get-tuple-element.9), channel_id=1, source_target_pairs={{0,8},{8,16},{16,24},{1,9},{9,17},{17,25},{2,10},{10,18},{18,26},{... | collective-permute-start | bytes 307208 | tf_op jit(solution)/shard_map/ppermute | solution.py:460
  11.5 0.0 copy-done.10
  11.5 0.1 pad.5.clone
  11.6 0.0 copy-done.9
  11.6 0.0 copy-done.3
  11.6 0.0 copy-done.2
  11.6 0.0 copy-start.5
  11.6 38.1 %bin_cells.1 = f32[4096,128]{1,0:T(8,128)S(1)} custom-call(s32[192]{0:T(256)S(1)} %add.37.dest_ref, f32[192,2048]{1,0:T(8,128)S(1)} %copy-done.2, s32[192,2048]{1,0:T(8,128)S(1)} %copy-done.3), custom_call_target="tpu_custom_call" | custom-call | flops 9663676416 | bytes 41943040 | tf_op jit(solution)/shard_map/bin_cells/pallas_call | solution.py:60
  49.8 0.0 copy-start.1
  49.8 0.0 collective-permute-done
  49.8 0.0 collective-permute-done.1
  49.9 0.0 copy-done.5
  49.9 1.4 pad_maximum_fusion.1
  51.3 0.0 copy-done.1
  51.3 3.5 %fusion = (f32[5,8,144,5]{3,2,1,0:T(8,128)}, f32[5,8,144,5]{3,2,1,0:T(8,128)}) fusion(f32[5,8,144,128]{3,2,1,0:T(8,128)S(1)} %pad_maximum_fusion.1), kind=kLoop, calls=%fused_computation.13 | loop fusion | bytes 460800 | tf_op jit(solution)/shard_map/slice | solution.py:459
  54.8 4.0 %copy.11 = f32[5,8,144,5]{2,1,3,0:T(8,128)} copy(f32[5,8,144,5]{3,2,1,0:T(8,128)} %get-tuple-element.6) | data formatting | bytes 230400 | tf_op jit(solution)/shard_map/slice | solution.py:459
  58.8 1.3 collective-permute-start.2
  60.1 4.0 %copy.12 = f32[5,8,144,5]{2,1,3,0:T(8,128)} copy(f32[5,8,144,5]{3,2,1,0:T(8,128)} %get-tuple-element.7) | data formatting | bytes 230400 | tf_op jit(solution)/shard_map/slice | solution.py:458
  64.0 6.2 %collective-permute-start.3 = (f32[5,8,144,5]{2,1,3,0:T(8,128)}, f32[5,8,144,5]{2,1,3,0:T(8,128)}, u32[]{:S(2)}, u32[]{:S(2)}) collective-permute-start(f32[5,8,144,5]{2,1,3,0:T(8,128)} %copy.12), channel_id=1, source_target_pairs={{0,1},{1,2},{2,3},{3,4},{4,5},{5,6},{6,7},{8,9},{9,10},{10,11},{11... | collective-permute-start | bytes 345608 | tf_op jit(solution)/shard_map/ppermute | solution.py:460
  70.2 0.7 and_convert_fusion.mask_ref
  70.9 0.0 collective-permute-done.2
  70.9 3.3 %copy.13 = f32[5,8,144,5]{3,2,1,0:T(8,128)} copy(f32[5,8,144,5]{2,1,3,0:T(8,128)} %collective-permute-done.2) | data formatting | bytes 230400 | tf_op jit(solution)/shard_map/ppermute | solution.py:461
  74.2 0.8 collective-permute-done.3
  75.0 3.2 %copy.14 = f32[5,8,144,5]{3,2,1,0:T(8,128)} copy(f32[5,8,144,5]{2,1,3,0:T(8,128)} %collective-permute-done.3) | data formatting | bytes 230400 | tf_op jit(solution)/shard_map/ppermute | solution.py:460
  78.2 5.9 %pad_maximum_fusion.stack_ref = f32[5,8,144,256]{3,2,1,0:T(8,128)} fusion(f32[5,8,144,5]{3,2,1,0:T(8,128)} %copy.14, f32[5,8,144,5]{3,2,1,0:T(8,128)} %copy.13, f32[5,8,5,128]{3,2,1,0:T(8,128)} %collective-permute-done.1, f32[5,8,6,128]{3,2,1,0:T(8,128)S(1)} %broadcast_in_dim.8, f32[5,8,5,128]{3,2,1,0:T(8,128)S(1)} %collective-permute-done, ...), kind=kLoop, calls=%fused_computation | loop fusion | flops 8847360 | bytes 9078784 | tf_op jit(solution)/shard_map/concatenate | solution.py:465
  84.1 57.2 %sweeps.1 = (f32[8,128,128]{2,1,0:T(8,128)}, f32[32,128,128]{2,1,0:T(8,128)}) custom-call(f32[144,256]{1,0:T(8,128)} %and_convert_fusion.mask_ref, f32[5,8,144,256]{3,2,1,0:T(8,128)} %pad_maximum_fusion.stack_ref, f32[32,128,128]{2,1,0:T(8,128)} %bitcast.12), custom_call_target="tpu_custom_call" | custom-call | tf_op jit(solution)/shard_map/sweeps/pallas_call | solution.py:419
  141.3 0.0 copy-start
  141.3 1.6 copy-done
  142.9 0.0 copy-start.8
  142.9 23.6 %cell_grads.1 = f32[2,192,2048]{2,1,0:T(8,128)} custom-call(s32[192]{0:T(256)S(1)} %add.37.dest_ref, f32[192,2048]{1,0:T(8,128)S(1)} %copy-done.2, s32[192,2048]{1,0:T(8,128)S(1)} %copy-done.3, f32[32,128,128]{2,1,0:T(8,128)S(1)} %copy-done), custom_call_target="tpu_custom_call" | custom-call | tf_op jit(solution)/shard_map/cell_grads/pallas_call | solution.py:134
  166.5 0.0 copy-done.8
  166.5 0.8 copy.20
  (8 shorter events, 0.1 us)
Async XLA Ops:
  0.6 3.6 %copy-start.6 = (f32[8,128,128]{2,1,0:T(8,128)S(1)}, f32[8,128,128]{2,1,0:T(8,128)}, u32[]{:S(2)}) copy-start(f32[8,128,128]{2,1,0:T(8,128)} %param.16) | copy-start | bytes 1572868
  0.6 3.7 %copy-start.7 = (f32[8,128,128]{2,1,0:T(8,128)S(1)}, f32[8,128,128]{2,1,0:T(8,128)}, u32[]{:S(2)}) copy-start(f32[8,128,128]{2,1,0:T(8,128)} %param.17) | copy-start | bytes 1572868
  0.7 10.9 %copy-start.10 = (s32[192,1]{0,1:T(1,128)S(1)}, s32[192,1]{0,1:T(1,128)}, u32[]{:S(2)}) copy-start(s32[192,1]{0,1:T(1,128)} %param.11) | copy-start | bytes 2308
  0.7 11.0 %copy-start.9 = (s32[192]{0:T(256)S(1)}, s32[192]{0:T(256)}, u32[]{:S(2)}) copy-start(s32[192]{0:T(256)} %param.12) | copy-start | bytes 2308
  0.7 11.0 %copy-start.3 = (s32[192,2048]{1,0:T(8,128)S(1)}, s32[192,2048]{1,0:T(8,128)}, u32[]{:S(2)}) copy-start(s32[192,2048]{1,0:T(8,128)} %bin_ref.3) | copy-start | bytes 4718596
  0.7 10.9 %copy-start.2 = (f32[192,2048]{1,0:T(8,128)S(1)}, f32[192,2048]{1,0:T(8,128)}, u32[]{:S(2)}) copy-start(f32[192,2048]{1,0:T(8,128)} %power_ref.3) | copy-start | bytes 4718596
  4.4 1.5 copy-start.4
  6.5 43.3 %collective-permute-start = (f32[5,8,5,128]{3,2,1,0:T(8,128)}, f32[5,8,5,128]{3,2,1,0:T(8,128)S(1)}, u32[]{:S(2)}, u32[]{:S(2)}) collective-permute-start(f32[5,8,5,128]{3,2,1,0:T(8,128)} %get-tuple-element.8), channel_id=1, source_target_pairs={{8,0},{16,8},{24,16},{9,1},{17,9},{25,17},{10,2},{18,10},{26,18},{... | collective-permute-start | bytes 307208 | tf_op jit(solution)/shard_map/ppermute | solution.py:461
  7.8 42.0 %collective-permute-start.1 = (f32[5,8,5,128]{3,2,1,0:T(8,128)S(1)}, f32[5,8,5,128]{3,2,1,0:T(8,128)}, u32[]{:S(2)}, u32[]{:S(2)}) collective-permute-start(f32[5,8,5,128]{3,2,1,0:T(8,128)S(1)} %get-tuple-element.9), channel_id=1, source_target_pairs={{0,8},{8,16},{16,24},{1,9},{9,17},{17,25},{2,10},{10,18},{18,26},{... | collective-permute-start | bytes 307208 | tf_op jit(solution)/shard_map/ppermute | solution.py:460
  11.6 38.2 %copy-start.5 = (f32[5,8,128,128]{3,2,1,0:T(8,128)S(1)}, f32[5,8,128,128]{3,2,1,0:T(8,128)}, u32[]{:S(2)}) copy-start(f32[5,8,128,128]{3,2,1,0:T(8,128)} %copy-done.4) | copy-start | bytes 7864324
  49.8 1.5 copy-start.1
  58.8 12.2 %collective-permute-start.2 = (f32[5,8,144,5]{2,1,3,0:T(8,128)}, f32[5,8,144,5]{2,1,3,0:T(8,128)}, u32[]{:S(2)}, u32[]{:S(2)}) collective-permute-start(f32[5,8,144,5]{2,1,3,0:T(8,128)} %copy.11), channel_id=1, source_target_pairs={{1,0},{2,1},{3,2},{4,3},{5,4},{6,5},{7,6},{9,8},{10,9},{11,10},{12... | collective-permute-start | bytes 345608 | tf_op jit(solution)/shard_map/ppermute | solution.py:461
  64.0 11.0 %collective-permute-start.3 = (f32[5,8,144,5]{2,1,3,0:T(8,128)}, f32[5,8,144,5]{2,1,3,0:T(8,128)}, u32[]{:S(2)}, u32[]{:S(2)}) collective-permute-start(f32[5,8,144,5]{2,1,3,0:T(8,128)} %copy.12), channel_id=1, source_target_pairs={{0,1},{1,2},{2,3},{3,4},{4,5},{5,6},{6,7},{8,9},{9,10},{10,11},{11... | collective-permute-start | bytes 345608 | tf_op jit(solution)/shard_map/ppermute | solution.py:460
  141.3 1.6 copy-start
  142.9 23.6 %copy-start.8 = (f32[8,128,128]{2,1,0:T(8,128)S(1)}, f32[8,128,128]{2,1,0:T(8,128)}, u32[]{:S(2)}) copy-start(f32[8,128,128]{2,1,0:T(8,128)} %get-tuple-element.12) | copy-start | bytes 1572868

commit v3 on v2

--- a/solution.py
+++ b/solution.py
@@ -11,6 +11,7 @@
 GROUP = 8
 HALO = 5
 PAD_ROWS = 16
+SLOT = 8
 VMEM_LIMIT = 48 * 1024 * 1024
 
 
@@ -25,19 +26,19 @@
 
     power = power_ref[...]
     bins = bin_ref[...]
-    high = power.astype(jnp.bfloat16).astype(jnp.float32)
-    low = power - high
+    high = power.astype(jnp.bfloat16)
+    low = (power - high.astype(jnp.float32)).astype(jnp.bfloat16)
     col = lax.bitwise_and(bins, cols - 1)
     row = lax.shift_right_logical(bins, cols.bit_length() - 1)
-    col = col.astype(jnp.float32)
-    row = row.astype(jnp.float32)
+    col = col.astype(jnp.float32).astype(jnp.bfloat16)
+    row = row.astype(jnp.float32).astype(jnp.bfloat16)
     col_iota = lax.broadcasted_iota(jnp.int32, (cols, cells), 0).astype(jnp.float32).astype(jnp.bfloat16)
     row_iota = lax.broadcasted_iota(jnp.int32, (TROWS, cells), 0).astype(jnp.float32).astype(jnp.bfloat16)
     one = jnp.ones((), jnp.bfloat16)
     zero = jnp.zeros((), jnp.bfloat16)
     for s in range(GROUP):
         def spread(x, n):
-            return jnp.broadcast_to(x[s : s + 1, :], (n, cells)).astype(jnp.bfloat16)
+            return jnp.broadcast_to(x[s : s + 1, :], (n, cells))
 
         col_hot = jnp.where(spread(col, cols) == col_iota, one, zero)
         row_mask = spread(row, TROWS) == row_iota
@@ -169,7 +170,11 @@
     size_gx,
     size_gy,
     mask_ref,
-    stack_ref,
+    temp_ref,
+    cond_x_ref,
+    cond_y_ref,
+    cond_z_ref,
+    weight_ref,
     partial_ref,
     temp_out,
     sens_out,
@@ -186,6 +191,12 @@
     sides,
     power_s,
     sens,
+    stack_ref,
+    row_bufs,
+    packed,
+    got,
+    row_sems,
+    col_sems,
     core_sems,
     x_sems,
     y_sems,
@@ -194,7 +205,7 @@
     back_x,
     back_core,
 ):
-    layers = stack_ref.shape[1]
+    layers = temp_ref.shape[0]
     _, rows, cols = partial_ref.shape
     size_x = size_gx // 2
     gx, gy = lax.axis_index("gx"), lax.axis_index("gy")
@@ -252,7 +263,80 @@
         for t in range(size_x):
             to_core(chunk(k), t).start()
 
+    args = (temp_ref, cond_x_ref, cond_y_ref, cond_z_ref, weight_ref)
+    up, down = lax.rem(gx + 1, size_gx), lax.rem(gx + size_gx - 1, size_gx)
+    arg_rows = []
+    for k, ref in enumerate(args):
+        arg_rows.append(
+            remote(ref.at[:, pl.ds(rows - 8, 8)], row_bufs.at[0, k], row_sems, (0, k), (up, gy))
+        )
+        arg_rows.append(remote(ref.at[:, pl.ds(0, 8)], row_bufs.at[1, k], row_sems, (1, k), (down, gy)))
+    for copy in arg_rows:
+        copy.start()
     loop(size_gy, send_core)
+    for k, ref in enumerate(args):
+        for l in range(layers):
+            stack_ref[k, l, :rows, :cols] = ref[l]
+    for copy in arg_rows:
+        copy.wait()
+    for k in range(len(args)):
+        for l in range(layers):
+            stack_ref[k, l, rows : rows + 8, :cols] = jnp.where(gx < size_gx - 1, row_bufs[1, k, l], 0.0)
+            stack_ref[k, l, rows + 8 :, :cols] = jnp.where(gx > 0, row_bufs[0, k, l], 0.0)
+    slots = cols // SLOT
+    slot_id = lax.broadcasted_iota(jnp.int32, wide.shape, 1) // SLOT
+    for q in range(packed.shape[1]):
+        to_left = jnp.zeros(wide.shape, jnp.float32)
+        to_right = jnp.zeros(wide.shape, jnp.float32)
+        for m in range(slots):
+            k, l = divmod(q * slots + m, layers)
+            if k < len(args):
+                turned = roll(stack_ref[k, l, :, :cols], SLOT * m, 1)
+                to_left = jnp.where(slot_id == m, turned, to_left)
+                to_right = jnp.where(slot_id == (m - 1) % slots, turned, to_right)
+        packed[0, q] = to_right
+        packed[1, q] = to_left
+    arg_cols = (
+        remote(packed.at[0], got.at[0], col_sems, (0,), (gx, ahead(1))),
+        remote(packed.at[1], got.at[1], col_sems, (1,), (gx, behind(1))),
+    )
+    for copy in arg_cols:
+        copy.start()
+
+    def send_x(k):
+        dj = chunk(k)
+        for t in range(size_x):
+            to_core(dj, t).wait_recv()
+            core_buf[t, dj] += partial_ref[(t * 2 + core) * size_gy + ahead(dj)]
+        for d in range(1, size_x):
+            to_x(dj, d).start()
+
+    loop(size_gy, send_x)
+
+    def add_x(dj):
+        total = core_buf[x, dj]
+        for d in range(1, size_x):
+            to_x(dj, d).wait_recv()
+            total = total + x_buf[d - 1, dj]
+        x_sum[dj] = total
+
+    def send_y(dj):
+        add_x(dj)
+        to_y(dj).start()
+
+    loop(size_gy, send_y, 1)
+    add_x(0)
+    for copy in arg_cols:
+        copy.wait()
+    for q in range(packed.shape[1]):
+        from_left = jnp.where(gy > 0, got[0, q], 0.0)
+        from_right = jnp.where(gy < size_gy - 1, got[1, q], 0.0)
+        for m in range(slots):
+            k, l = divmod(q * slots + m, layers)
+            if k < len(args):
+                both = jnp.where(slot_id == m, from_right, 0.0)
+                both = jnp.where(slot_id == (m - 1) % slots, from_left, both)
+                stack_ref[k, l, :, cols:] = roll(both, -SLOT * m, 1)
 
     mask = mask_ref[...]
     for l in range(layers):
@@ -267,29 +351,6 @@
         south_s[l] = south
         inv_s[l] = jnp.where(mask > 0.0, 1.0 / diag, 0.0)
 
-    def send_x(k):
-        dj = chunk(k)
-        for t in range(size_x):
-            to_core(dj, t).wait_recv()
-            core_buf[t, dj] += partial_ref[(t * 2 + core) * size_gy + ahead(dj)]
-        for d in range(1, size_x):
-            to_x(dj, d).start()
-
-    loop(size_gy, send_x)
-
-    def add_x(dj):
-        total = core_buf[x, dj]
-        for d in range(1, size_x):
-            to_x(dj, d).wait_recv()
-            total = total + x_buf[d - 1, dj]
-        x_sum[dj] = total
-
-    def send_y(dj):
-        add_x(dj)
-        to_y(dj).start()
-
-    loop(size_gy, send_y, 1)
-    add_x(0)
     wide[:rows] = x_sum[0]
 
     def add_y(dj):
@@ -298,7 +359,6 @@
 
     loop(size_gy, add_y, 1)
 
-    up, down = lax.rem(gx + 1, size_gx), lax.rem(gx + size_gx - 1, size_gx)
     halo_rows = (
         remote(wide.at[pl.ds(rows - 8, 8)], wide.at[pl.ds(rows + 8, 8)], halo_sems, (0,), (up, gy)),
         remote(wide.at[pl.ds(0, 8)], wide.at[pl.ds(rows, 8)], halo_sems, (1,), (down, gy)),
@@ -404,9 +464,11 @@
     loop(size_gx * size_gy, store)
 
 
-def sweeps(mask, stack, partial, size_gx, size_gy):
+def sweeps(mask, args, partial, size_gx, size_gy):
     owners, rows, cols = partial.shape
-    _, layers, wide_rows, wide_cols = stack.shape
+    layers = args[0].shape[0]
+    wide_rows, wide_cols = mask.shape
+    buffers = -(-len(args) * layers * SLOT // cols)
     size_x = size_gx // 2
     vmem = pl.BlockSpec(memory_space=pltpu.VMEM)
 
@@ -422,7 +484,7 @@
             jax.ShapeDtypeStruct((layers, rows, cols), jnp.float32),
             jax.ShapeDtypeStruct((owners, rows, cols), jnp.float32),
         ),
-        in_specs=[vmem] * 3,
+        in_specs=[vmem] * (2 + len(args)),
         out_specs=(vmem, vmem),
         scratch_shapes=[pltpu.VMEM((layers, wide_rows, wide_cols), jnp.float32)] * 5
         + [
@@ -434,6 +496,12 @@
             blocks(2, length=wide_rows),
             pltpu.VMEM((wide_rows, wide_cols), jnp.float32),
             blocks(owners),
+            pltpu.VMEM((len(args), layers, wide_rows, wide_cols), jnp.float32),
+            blocks(2, len(args), layers, length=8),
+            blocks(2, buffers, length=wide_rows),
+            blocks(2, buffers, length=wide_rows),
+            sems(2, len(args)),
+            sems(2),
             sems(size_x, size_gy),
             sems(size_x - 1, size_gy),
             sems(size_gy - 1),
@@ -446,24 +514,7 @@
             vmem_limit_bytes=56 * 1024 * 1024, collective_id=0, has_side_effects=True
         ),
         name="sweeps",
-    )(mask, stack, partial)
-
-
-def padded(array, width, row_dim):
-    for axis, dim, room in (("gx", row_dim, PAD_ROWS), ("gy", row_dim + 1, array.shape[row_dim + 1])):
-        peers = lax.axis_size(axis)
-        length = array.shape[dim] if dim == row_dim else room
-        up = [(i, i + 1) for i in range(peers - 1)]
-        down = [(j, i) for i, j in up]
-        last = lax.slice_in_dim(array, length - width, length, axis=dim)
-        first = lax.slice_in_dim(array, 0, width, axis=dim)
-        before = lax.ppermute(last, axis, up)
-        after = lax.ppermute(first, axis, down)
-        shape = list(array.shape)
-        shape[dim] = room - 2 * width
-        gap = jnp.zeros(shape, array.dtype)
-        array = jnp.concatenate([array, after, gap, before], axis=dim)
-    return array
+    )(mask, *args, partial)
 
 
 def inside_mask(rows, cols):
@@ -486,11 +537,11 @@
     size_gx, size_gy = lax.axis_size("gx"), lax.axis_size("gy")
     devices = size_gx * size_gy
     dest = block_owner[:, 0] * tiles + block_tile
-    stack = padded(jnp.stack([temp_prev, cond_x, cond_y, cond_z, weight]), HALO, 2)
+    args = (temp_prev, cond_x, cond_y, cond_z, weight)
     mask = inside_mask(rows, cols)
     partial = bin_cells(dest, cell_power, cell_bin, devices * rows, cols)
     partial = partial.reshape(devices, rows, cols)
-    temperature, sens = sweeps(mask, stack, partial, size_gx, size_gy)
+    temperature, sens = sweeps(mask, args, partial, size_gx, size_gy)
     grads = cell_grads(dest, cell_power, cell_bin, sens, size_gx, size_gy)
     return temperature, grads
 

time: 170 us -> 135 us (0.79)
  local copies, waits for them, and re-layouts: 26.2 us -> 6.53 us
  starting transfers between devices: 12.4 us -> 0 us
  other arithmetic: 8.05 us -> 2.14 us
  Pallas kernels: 119 us -> 123 us
    ppermute x4 -> x0, starting transfers between devices: 12.4 us -> none  [the longest x2 9.87 us: padded(): before = lax.ppermute(last, axis, up)]
    slice x4 -> x0, local copies, waits for them, and re-layouts: 12.2 us -> none  [the longest x3 8.2 us: padded(): first = lax.slice_in_dim(array, 0, width, axis=dim)]
    concatenate x2 -> x0, other arithmetic: 7.28 us -> none  [padded(): array = jnp.concatenate([array, after, gap, before], axis=dim)]
    ppermute x2 -> x0, local copies, waits for them, and re-layouts: 6.44 us -> none  [the longest x1 3.27 us: padded(): after = lax.ppermute(first, axis, down)]
    pallas_call x1, Pallas kernels: 57.2 us -> 61.6 us  [sweeps(): pl.pallas_call(functools.partial(sweep_kernel, size_gx, size_gy), out_sha...]
    unnamed x27 -> x15, local copies, waits for them, and re-layouts: 7.46 us -> 6.53 us
  transfers between devices with their start and end apart: 4 -> 0, of which waited for: 1 -> 0; matrix products, arithmetic and copies ran while one was open for 5% -> 0% of each run, Pallas kernels for 23% -> 0%
where the time goes in v3:
time: 135 us; the launch traced here: 133 us
  Pallas kernels  123 us (91%)
  local copies, waits for them, and re-layouts  6.53 us (5%)
  other arithmetic  2.14 us (2%)
    pallas_call x1, Pallas kernels, sweeps(): pl.pallas_call(functools.partial(sweep_kernel, size_gx, size_gy), out_sha...  61.6 us
    pallas_call x1, Pallas kernels, bin_cells(): pl.pallas_call(bin_kernel, grid_spec=pltpu.PrefetchScalarGridSpec(num_sca...  38.1 us
    pallas_call x1, Pallas kernels, cell_grads(): pl.pallas_call(functools.partial(grad_kernel, size_gx, size_gy), grid_spe...  23.6 us
    unnamed x15, local copies, waits for them, and re-layouts  6.53 us

profile of v3, /device:TPU:0, one launch (start us, length us, event | category | flops | bytes accessed | tf_op | source)
XLA Modules:
  0.0 132.7 jit_solution(16712401962715602005)
XLA Ops:
  0.7 0.7 broadcast_multiply_fusion
  1.4 0.7 add.37.dest_ref
  2.0 0.7 and_convert_fusion.mask_ref
  2.8 0.0 copy-start.2
  2.8 1.4 %copy-done.2 = f32[192,2048]{1,0:T(8,128)S(1)} copy-done((f32[192,2048]{1,0:T(8,128)S(1)}, f32[192,2048]{1,0:T(8,128)}, u32[]{:S(2)}) %copy-start.2) | copy-done | bytes 1572888
  4.2 0.0 copy-start.4
  4.2 1.4 %copy-done.4 = s32[192,2048]{1,0:T(8,128)S(1)} copy-done((s32[192,2048]{1,0:T(8,128)S(1)}, s32[192,2048]{1,0:T(8,128)}, u32[]{:S(2)}) %copy-start.4) | copy-done | bytes 1572888
  5.6 38.1 %bin_cells.1 = f32[4096,128]{1,0:T(8,128)S(1)} custom-call(s32[192]{0:T(256)S(1)} %add.37.dest_ref, f32[192,2048]{1,0:T(8,128)S(1)} %copy-done.2, s32[192,2048]{1,0:T(8,128)S(1)} %copy-done.4), custom_call_target="tpu_custom_call" | custom-call | flops 9663676416 | bytes 41943040 | tf_op jit(solution)/shard_map/bin_cells/pallas_call | solution.py:61
  43.7 0.0 copy-start.1
  43.7 1.3 %copy-done.1 = f32[4096,128]{1,0:T(8,128)} copy-done((f32[4096,128]{1,0:T(8,128)}, f32[4096,128]{1,0:T(8,128)S(1)}, u32[]{:S(2)}) %copy-start.1) | copy-done | bytes 2097176
  45.1 0.0 copy-start.3
  45.1 0.0 copy-start.5
  45.1 61.6 %sweeps.1 = (f32[8,128,128]{2,1,0:T(8,128)}, f32[32,128,128]{2,1,0:T(8,128)}) custom-call(f32[144,256]{1,0:T(8,128)} %and_convert_fusion.mask_ref, f32[8,128,128]{2,1,0:T(8,128)} %temp_ref.1, f32[8,128,128]{2,1,0:T(8,128)} %cond_x_ref.1, f32[8,128,128]{2,1,0:T(8,128)} %cond_y_ref.1, f32[8,128,128]{2,1,0:T(8,128)} %cond_z_ref.1, f32[8,128,128]{2,1,0:T(8,128)} %weight_ref.1, ...), custom_call_target="tpu_custom_call" | custom-call | tf_op jit(solution)/shard_map/sweeps/pallas_call | solution.py:481
  106.7 0.0 copy-done.3
  106.7 0.0 copy-done.5
  106.7 0.0 copy-start
  106.7 1.6 %copy-done = f32[32,128,128]{2,1,0:T(8,128)S(1)} copy-done((f32[32,128,128]{2,1,0:T(8,128)S(1)}, f32[32,128,128]{2,1,0:T(8,128)}, u32[]{:S(2)}) %copy-start) | copy-done | bytes 2097176
  108.3 0.0 copy-start.6
  108.3 23.6 %cell_grads.1 = f32[2,192,2048]{2,1,0:T(8,128)} custom-call(s32[192]{0:T(256)S(1)} %add.37.dest_ref, f32[192,2048]{1,0:T(8,128)S(1)} %copy-done.3, s32[192,2048]{1,0:T(8,128)S(1)} %copy-done.5, f32[32,128,128]{2,1,0:T(8,128)S(1)} %copy-done), custom_call_target="tpu_custom_call" | custom-call | tf_op jit(solution)/shard_map/cell_grads/pallas_call | solution.py:135
  131.9 0.0 copy-done.6
  131.9 0.8 copy.12
  (2 shorter events, 0.0 us)
Async XLA Ops:
  2.8 1.4 %copy-start.2 = (f32[192,2048]{1,0:T(8,128)S(1)}, f32[192,2048]{1,0:T(8,128)}, u32[]{:S(2)}) copy-start(f32[192,2048]{1,0:T(8,128)} %power_ref.3) | copy-start | bytes 4718596
  4.2 1.4 %copy-start.4 = (s32[192,2048]{1,0:T(8,128)S(1)}, s32[192,2048]{1,0:T(8,128)}, u32[]{:S(2)}) copy-start(s32[192,2048]{1,0:T(8,128)} %bin_ref.3) | copy-start | bytes 4718596
  43.7 1.3 %copy-start.1 = (f32[4096,128]{1,0:T(8,128)}, f32[4096,128]{1,0:T(8,128)S(1)}, u32[]{:S(2)}) copy-start(f32[4096,128]{1,0:T(8,128)S(1)} %bin_cells.1) | copy-start | bytes 6291460
  45.1 61.6 %copy-start.3 = (f32[192,2048]{1,0:T(8,128)S(1)}, f32[192,2048]{1,0:T(8,128)}, u32[]{:S(2)}) copy-start(f32[192,2048]{1,0:T(8,128)} %power_ref.3) | copy-start | bytes 4718596
  45.1 61.6 %copy-start.5 = (s32[192,2048]{1,0:T(8,128)S(1)}, s32[192,2048]{1,0:T(8,128)}, u32[]{:S(2)}) copy-start(s32[192,2048]{1,0:T(8,128)} %bin_ref.3) | copy-start | bytes 4718596
  106.7 1.6 %copy-start = (f32[32,128,128]{2,1,0:T(8,128)S(1)}, f32[32,128,128]{2,1,0:T(8,128)}, u32[]{:S(2)}) copy-start(f32[32,128,128]{2,1,0:T(8,128)} %get-tuple-element.5.sens_ref) | copy-start | bytes 6291460
  108.3 23.6 %copy-start.6 = (f32[8,128,128]{2,1,0:T(8,128)S(1)}, f32[8,128,128]{2,1,0:T(8,128)}, u32[]{:S(2)}) copy-start(f32[8,128,128]{2,1,0:T(8,128)} %get-tuple-element.8) | copy-start | bytes 1572868

commit v4 on v3

--- a/solution.py
+++ b/solution.py
@@ -9,6 +9,8 @@
 
 TROWS = 16
 GROUP = 8
+BATCH = 32
+PARTS = 2
 HALO = 5
 PAD_ROWS = 16
 SLOT = 8
@@ -24,36 +26,44 @@
     def _():
         map_ref[...] = jnp.zeros_like(map_ref)
 
-    power = power_ref[...]
-    bins = bin_ref[...]
-    high = power.astype(jnp.bfloat16)
-    low = (power - high.astype(jnp.float32)).astype(jnp.bfloat16)
-    col = lax.bitwise_and(bins, cols - 1)
-    row = lax.shift_right_logical(bins, cols.bit_length() - 1)
-    col = col.astype(jnp.float32).astype(jnp.bfloat16)
-    row = row.astype(jnp.float32).astype(jnp.bfloat16)
-    col_iota = lax.broadcasted_iota(jnp.int32, (cols, cells), 0).astype(jnp.float32).astype(jnp.bfloat16)
-    row_iota = lax.broadcasted_iota(jnp.int32, (TROWS, cells), 0).astype(jnp.float32).astype(jnp.bfloat16)
-    one = jnp.ones((), jnp.bfloat16)
-    zero = jnp.zeros((), jnp.bfloat16)
-    for s in range(GROUP):
-        def spread(x, n):
-            return jnp.broadcast_to(x[s : s + 1, :], (n, cells))
-
-        col_hot = jnp.where(spread(col, cols) == col_iota, one, zero)
-        row_mask = spread(row, TROWS) == row_iota
-        left = jnp.concatenate(
-            [
-                jnp.where(row_mask, spread(high, TROWS), zero),
-                jnp.where(row_mask, spread(low, TROWS), zero),
-            ],
-            axis=0,
-        )
-        tile = lax.dot_general(
-            left, col_hot, (((1,), (1,)), ((), ())), preferred_element_type=jnp.float32
-        )
-        start = pl.multiple_of(dest_ref[step * GROUP + s] * TROWS, TROWS)
-        map_ref[pl.ds(start, TROWS), :] += tile[:TROWS] + tile[TROWS:]
+    for g in range(power_ref.shape[0] // GROUP):
+        at = slice(g * GROUP, (g + 1) * GROUP)
+        first = step * power_ref.shape[0] + g * GROUP
+        power = power_ref[at, :]
+        bins = bin_ref[at, :]
+        high = power.astype(jnp.bfloat16)
+        low = (power - high.astype(jnp.float32)).astype(jnp.bfloat16)
+        narrow = cols // PARTS
+        col = lax.bitwise_and(bins, narrow - 1)
+        row = lax.shift_right_logical(bins, narrow.bit_length() - 1)
+        col = col.astype(jnp.float32).astype(jnp.bfloat16)
+        row = row.astype(jnp.float32).astype(jnp.bfloat16)
+        col_iota = lax.broadcasted_iota(jnp.int32, (narrow, cells), 0).astype(jnp.float32).astype(jnp.bfloat16)
+        line = lax.broadcasted_iota(jnp.int32, (TROWS * PARTS, cells), 0)
+        line = lax.rem(line, TROWS) * PARTS + line // TROWS
+        row_iota = line.astype(jnp.float32).astype(jnp.bfloat16)
+        one = jnp.ones((), jnp.bfloat16)
+        zero = jnp.zeros((), jnp.bfloat16)
+        for s in range(GROUP):
+            def spread(x, n):
+                return jnp.broadcast_to(x[s : s + 1, :], (n, cells))
+
+            col_hot = jnp.where(spread(col, narrow) == col_iota, one, zero)
+            row_mask = spread(row, TROWS * PARTS) == row_iota
+            left = jnp.concatenate(
+                [
+                    jnp.where(row_mask, spread(high, TROWS * PARTS), zero),
+                    jnp.where(row_mask, spread(low, TROWS * PARTS), zero),
+                ],
+                axis=0,
+            )
+            tile = lax.dot_general(
+                left, col_hot, (((1,), (1,)), ((), ())), preferred_element_type=jnp.float32
+            )
+            start = pl.multiple_of(dest_ref[first + s] * TROWS, TROWS)
+            tile = tile[: TROWS * PARTS] + tile[TROWS * PARTS :]
+            tile = [tile[p * TROWS : (p + 1) * TROWS] for p in range(PARTS)]
+            map_ref[pl.ds(start, TROWS), :] += jnp.concatenate(tile, axis=1)
 
 
 def bin_cells(dest, cell_power, cell_bin, map_rows, cols):
@@ -62,8 +72,8 @@
         bin_kernel,
         grid_spec=pltpu.PrefetchScalarGridSpec(
             num_scalar_prefetch=1,
-            grid=(blocks // GROUP,),
-            in_specs=[pl.BlockSpec((GROUP, cells), lambda i, d: (i, 0))] * 2,
+            grid=(blocks // BATCH,),
+            in_specs=[pl.BlockSpec((BATCH, cells), lambda i, d: (i, 0))] * 2,
             out_specs=pl.BlockSpec((map_rows, cols), lambda i, d: (0, 0)),
         ),
         out_shape=jax.ShapeDtypeStruct((map_rows, cols), jnp.float32),
@@ -108,25 +118,28 @@
 
         lax.fori_loop(0, owners, one, 0)
 
-    for s in range(GROUP):
-        start = pl.multiple_of(dest_ref[step * GROUP + s] * TROWS, TROWS)
-        for a in range(2):
-            table_ref[a, :, s, :] = slope_ref[a, pl.ds(start, TROWS), :]
-    for c in range(cells // cols):
-        at = slice(c * cols, (c + 1) * cols)
-        bins = bin_ref[:, at]
-        power = power_ref[:, at]
-        col = lax.bitwise_and(bins, cols - 1)
-        row = lax.shift_right_logical(bins, cols.bit_length() - 1)
-        masks = [lax.bitwise_and(row, 1 << b) != 0 for b in range(4)]
-        for a in range(2):
-            picks = [
-                jnp.take_along_axis(table_ref[a, r], col, axis=1, mode="promise_in_bounds")
-                for r in range(TROWS)
-            ]
-            for mask in masks:
-                picks = [jnp.where(mask, picks[2 * k + 1], picks[2 * k]) for k in range(len(picks) // 2)]
-            out_ref[a, :, at] = picks[0] * power
+    for g in range(power_ref.shape[0] // GROUP):
+        lines = slice(g * GROUP, (g + 1) * GROUP)
+        first = step * power_ref.shape[0] + g * GROUP
+        for s in range(GROUP):
+            start = pl.multiple_of(dest_ref[first + s] * TROWS, TROWS)
+            for a in range(2):
+                table_ref[g, a, :, s, :] = slope_ref[a, pl.ds(start, TROWS), :]
+        for c in range(cells // cols):
+            at = slice(c * cols, (c + 1) * cols)
+            bins = bin_ref[lines, at]
+            power = power_ref[lines, at]
+            col = lax.bitwise_and(bins, cols - 1)
+            row = lax.shift_right_logical(bins, cols.bit_length() - 1)
+            masks = [lax.bitwise_and(row, 1 << b) != 0 for b in range(4)]
+            for a in range(2):
+                picks = [
+                    jnp.take_along_axis(table_ref[g, a, r], col, axis=1, mode="promise_in_bounds")
+                    for r in range(TROWS)
+                ]
+                for mask in masks:
+                    picks = [jnp.where(mask, picks[2 * k + 1], picks[2 * k]) for k in range(len(picks) // 2)]
+                out_ref[a, lines, at] = picks[0] * power
 
 
 def cell_grads(dest, cell_power, cell_bin, sens, size_gx, size_gy):
@@ -136,13 +149,13 @@
         functools.partial(grad_kernel, size_gx, size_gy),
         grid_spec=pltpu.PrefetchScalarGridSpec(
             num_scalar_prefetch=1,
-            grid=(blocks // GROUP,),
-            in_specs=[pl.BlockSpec((GROUP, cells), lambda i, d: (i, 0))] * 2
+            grid=(blocks // BATCH,),
+            in_specs=[pl.BlockSpec((BATCH, cells), lambda i, d: (i, 0))] * 2
             + [pl.BlockSpec((owners, rows, cols), lambda i, d: (0, 0, 0))],
-            out_specs=pl.BlockSpec((2, GROUP, cells), lambda i, d: (0, i, 0)),
+            out_specs=pl.BlockSpec((2, BATCH, cells), lambda i, d: (0, i, 0)),
             scratch_shapes=[
                 pltpu.VMEM((2, owners * rows, cols), jnp.float32),
-                pltpu.VMEM((2, TROWS, GROUP, cols), jnp.float32),
+                pltpu.VMEM((BATCH // GROUP, 2, TROWS, GROUP, cols), jnp.float32),
             ],
         ),
         out_shape=jax.ShapeDtypeStruct((2, blocks, cells), jnp.float32),

time: 135 us -> 110 us (0.81)
  Pallas kernels: 123 us -> 98.1 us
    pallas_call x1, Pallas kernels: 38.1 us -> 15.1 us  [bin_cells(): pl.pallas_call(bin_kernel, grid_spec=pltpu.PrefetchScalarGridSpec(num_sca...]
    pallas_call x1, Pallas kernels: 23.6 us -> 21.4 us  [cell_grads(): pl.pallas_call(functools.partial(grad_kernel, size_gx, size_gy), grid_spe...]
where the time goes in v4:
time: 110 us; the launch traced here: 107 us
  Pallas kernels  98.1 us (89%)
  local copies, waits for them, and re-layouts  6.56 us (6%)
  other arithmetic  2.14 us (2%)
    pallas_call x1, Pallas kernels, sweeps(): pl.pallas_call(functools.partial(sweep_kernel, size_gx, size_gy), out_sha...  61.6 us
    pallas_call x1, Pallas kernels, cell_grads(): pl.pallas_call(functools.partial(grad_kernel, size_gx, size_gy), grid_spe...  21.4 us
    pallas_call x1, Pallas kernels, bin_cells(): pl.pallas_call(bin_kernel, grid_spec=pltpu.PrefetchScalarGridSpec(num_sca...  15.1 us
    unnamed x15, local copies, waits for them, and re-layouts  6.56 us

profile of v4, /device:TPU:0, one launch (start us, length us, event | category | flops | bytes accessed | tf_op | source)
XLA Modules:
  0.0 107.5 jit_solution(229359395171133666)
XLA Ops:
  0.7 0.7 broadcast_multiply_fusion
  1.4 0.7 add.37.dest_ref
  2.0 0.7 and_convert_fusion.mask_ref
  2.8 0.0 copy-start.2
  2.8 1.4 %copy-done.2 = f32[192,2048]{1,0:T(8,128)S(1)} copy-done((f32[192,2048]{1,0:T(8,128)S(1)}, f32[192,2048]{1,0:T(8,128)}, u32[]{:S(2)}) %copy-start.2) | copy-done | bytes 1572888
  4.2 0.0 copy-start.4
  4.2 1.4 %copy-done.4 = s32[192,2048]{1,0:T(8,128)S(1)} copy-done((s32[192,2048]{1,0:T(8,128)S(1)}, s32[192,2048]{1,0:T(8,128)}, u32[]{:S(2)}) %copy-start.4) | copy-done | bytes 1572888
  5.6 15.1 %bin_cells.1 = f32[4096,128]{1,0:T(8,128)S(1)} custom-call(s32[192]{0:T(256)S(1)} %add.37.dest_ref, f32[192,2048]{1,0:T(8,128)S(1)} %copy-done.2, s32[192,2048]{1,0:T(8,128)S(1)} %copy-done.4), custom_call_target="tpu_custom_call" | custom-call | flops 9663676416 | bytes 41943040 | tf_op jit(solution)/shard_map/bin_cells/pallas_call | solution.py:71
  20.7 0.0 copy-start.1
  20.7 1.4 %copy-done.1 = f32[4096,128]{1,0:T(8,128)} copy-done((f32[4096,128]{1,0:T(8,128)}, f32[4096,128]{1,0:T(8,128)S(1)}, u32[]{:S(2)}) %copy-start.1) | copy-done | bytes 2097176
  22.1 0.0 copy-start.3
  22.1 0.0 copy-start.5
  22.1 61.6 %sweeps.1 = (f32[8,128,128]{2,1,0:T(8,128)}, f32[32,128,128]{2,1,0:T(8,128)}) custom-call(f32[144,256]{1,0:T(8,128)} %and_convert_fusion.mask_ref, f32[8,128,128]{2,1,0:T(8,128)} %temp_ref.1, f32[8,128,128]{2,1,0:T(8,128)} %cond_x_ref.1, f32[8,128,128]{2,1,0:T(8,128)} %cond_y_ref.1, f32[8,128,128]{2,1,0:T(8,128)} %cond_z_ref.1, f32[8,128,128]{2,1,0:T(8,128)} %weight_ref.1, ...), custom_call_target="tpu_custom_call" | custom-call | tf_op jit(solution)/shard_map/sweeps/pallas_call | solution.py:494
  83.7 0.0 copy-done.3
  83.7 0.0 copy-done.5
  83.7 0.0 copy-start
  83.7 1.6 %copy-done = f32[32,128,128]{2,1,0:T(8,128)S(1)} copy-done((f32[32,128,128]{2,1,0:T(8,128)S(1)}, f32[32,128,128]{2,1,0:T(8,128)}, u32[]{:S(2)}) %copy-start) | copy-done | bytes 2097176
  85.3 0.0 copy-start.6
  85.3 21.4 %cell_grads.1 = f32[2,192,2048]{2,1,0:T(8,128)} custom-call(s32[192]{0:T(256)S(1)} %add.37.dest_ref, f32[192,2048]{1,0:T(8,128)S(1)} %copy-done.3, s32[192,2048]{1,0:T(8,128)S(1)} %copy-done.5, f32[32,128,128]{2,1,0:T(8,128)S(1)} %copy-done), custom_call_target="tpu_custom_call" | custom-call | tf_op jit(solution)/shard_map/cell_grads/pallas_call | solution.py:148
  106.7 0.0 copy-done.6
  106.7 0.8 copy.12
  (2 shorter events, 0.0 us)
Async XLA Ops:
  2.8 1.4 %copy-start.2 = (f32[192,2048]{1,0:T(8,128)S(1)}, f32[192,2048]{1,0:T(8,128)}, u32[]{:S(2)}) copy-start(f32[192,2048]{1,0:T(8,128)} %power_ref.3) | copy-start | bytes 4718596
  4.2 1.4 %copy-start.4 = (s32[192,2048]{1,0:T(8,128)S(1)}, s32[192,2048]{1,0:T(8,128)}, u32[]{:S(2)}) copy-start(s32[192,2048]{1,0:T(8,128)} %bin_ref.3) | copy-start | bytes 4718596
  20.7 1.4 %copy-start.1 = (f32[4096,128]{1,0:T(8,128)}, f32[4096,128]{1,0:T(8,128)S(1)}, u32[]{:S(2)}) copy-start(f32[4096,128]{1,0:T(8,128)S(1)} %bin_cells.1) | copy-start | bytes 6291460
  22.1 61.6 %copy-start.3 = (f32[192,2048]{1,0:T(8,128)S(1)}, f32[192,2048]{1,0:T(8,128)}, u32[]{:S(2)}) copy-start(f32[192,2048]{1,0:T(8,128)} %power_ref.3) | copy-start | bytes 4718596
  22.1 61.6 %copy-start.5 = (s32[192,2048]{1,0:T(8,128)S(1)}, s32[192,2048]{1,0:T(8,128)}, u32[]{:S(2)}) copy-start(s32[192,2048]{1,0:T(8,128)} %bin_ref.3) | copy-start | bytes 4718596
  83.7 1.6 %copy-start = (f32[32,128,128]{2,1,0:T(8,128)S(1)}, f32[32,128,128]{2,1,0:T(8,128)}, u32[]{:S(2)}) copy-start(f32[32,128,128]{2,1,0:T(8,128)} %get-tuple-element.5.sens_ref) | copy-start | bytes 6291460
  85.3 21.4 %copy-start.6 = (f32[8,128,128]{2,1,0:T(8,128)S(1)}, f32[8,128,128]{2,1,0:T(8,128)}, u32[]{:S(2)}) copy-start(f32[8,128,128]{2,1,0:T(8,128)} %get-tuple-element.8) | copy-start | bytes 1572868
